TPU v7x, 32 devices: a whole 2x2x4 slice. The times are simulated.
32 devices in a mesh: dp: 8 (over y, x, core), seq: 4 (over z).
Axes of the slice: x: 2, y: 2, z: 4, core: 2. Of those that a mesh axis runs over, the one named last changes fastest.
Arguments:
- clips: bfloat16 [16, 8, 14, 14, 512], P('dp', 'seq'), may hold values from -6 to 6
- out_grad: bfloat16 [16, 8, 14, 14, 512], P('dp', 'seq'), may hold values from -6 to 6
- clip_order: int32 [8, 2], P('dp'), may hold values from 0 to 1, each once within a row
- region_label: int32 [4, 392], replicated, may hold values from 0 to 3
- rel_index: int32 [392, 392], replicated, may hold values from 0 to 2534
- norm1_gain: bfloat16 [512], P(('dp', 'seq')), may hold values from 0.5 to 1.5
- norm1_bias: bfloat16 [512], P(('dp', 'seq')), may hold values from -3 to 3
- qkv_weight: bfloat16 [512, 1536], P(('dp', 'seq')), may hold values from -0.25 to 0.25
- qv_bias: bfloat16 [2, 512], P(None, ('dp', 'seq')), may hold values from -3 to 3
- bias_table: bfloat16 [16, 2535], P('seq'), may hold values from -3 to 3
- proj_weight: bfloat16 [512, 512], P(('dp', 'seq')), may hold values from -1.5 to 1.5
- proj_bias: bfloat16 [512], P(('dp', 'seq')), may hold values from -3 to 3
- norm2_gain: bfloat16 [512], P(('dp', 'seq')), may hold values from 0.5 to 1.5
- norm2_bias: bfloat16 [512], P(('dp', 'seq')), may hold values from -3 to 3
- fc1_weight: bfloat16 [512, 2048], P(('dp', 'seq')), may hold values from -0.25 to 0.25
- fc1_bias: bfloat16 [2048], P(('dp', 'seq')), may hold values from -3 to 3
- fc2_weight: bfloat16 [2048, 512], P(('dp', 'seq')), may hold values from -0.1875 to 0.1875
- fc2_bias: bfloat16 [512], P(('dp', 'seq')), may hold values from -3 to 3
Outputs:
- output: bfloat16 [16, 8, 14, 14, 512], P('dp', 'seq')
- clips_grad: bfloat16 [16, 8, 14, 14, 512], P('dp', 'seq')
- norm1_gain_grad: float32 [512], P(('dp', 'seq'))
- norm1_bias_grad: float32 [512], P(('dp', 'seq'))
- qkv_weight_grad: float32 [512, 1536], P(('dp', 'seq'))
- qv_bias_grad: float32 [2, 512], P(None, ('dp', 'seq'))
- bias_table_grad: float32 [16, 2535], P('seq')
- proj_weight_grad: float32 [512, 512], P(('dp', 'seq'))
- proj_bias_grad: float32 [512], P(('dp', 'seq'))
- norm2_gain_grad: float32 [512], P(('dp', 'seq'))
- norm2_bias_grad: float32 [512], P(('dp', 'seq'))
- fc1_weight_grad: float32 [512, 2048], P(('dp', 'seq'))
- fc1_bias_grad: float32 [2048], P(('dp', 'seq'))
- fc2_weight_grad: float32 [2048, 512], P(('dp', 'seq'))
- fc2_bias_grad: float32 [512], P(('dp', 'seq'))
Inputs may be any that keep to these rules, and one draw needn't show every extreme that they name: `clip_order`: each row is a permutation of 0 to 1.
All inputs are finite; a program needn't handle non-finite values.
Results may differ from a plain program's by a relative error of at most 0.011.
Values may be sent and summed in bfloat16 or wider, within the bound.
A program may use at most 256 MiB of HBM per device.

v0:
```python
import functools
import math

import jax
import jax.numpy as jnp
import numpy as np
from jax import lax
from jax.experimental import pallas as pl
from jax.experimental.pallas import tpu as pltpu
from jax.sharding import PartitionSpec as P

HD = 32
WIN_T = 8
WIN_S = 7
SHIFT_T = 4
SHIFT_S = 3
FR = 8
SIDE = 14
MICRO = 2
NWIN = 4
WT = 392
TBL = 2535


eps_norm = 1e-05


def layer_norm(values, norm_gain, norm_shift):
    average = jnp.mean(values, axis=-1, keepdims=True)
    centred = values - average
    variance = jnp.mean(centred * centred, axis=-1, keepdims=True)
    return centred * lax.rsqrt(variance + eps_norm) * norm_gain + norm_shift


def gelu_exact(values):
    return jax.nn.gelu(values, approximate=False)


def matmul(left_side, right_side):
    return jnp.dot(left_side, right_side, preferred_element_type=jnp.float32)


def window_split(field):
    rolled = jnp.roll(field, (-SHIFT_T, -SHIFT_S, -SHIFT_S), (0, 1, 2))
    blocks = rolled.reshape(FR // WIN_T, WIN_T, SIDE // WIN_S, WIN_S, SIDE // WIN_S, WIN_S, -1)
    return blocks.transpose(0, 2, 4, 1, 3, 5, 6).reshape(NWIN, WT, -1)


def window_merge(windows):
    blocks = windows.reshape(FR // WIN_T, SIDE // WIN_S, SIDE // WIN_S, WIN_T, WIN_S, WIN_S, -1)
    field = blocks.transpose(0, 3, 1, 4, 2, 5, 6).reshape(FR, SIDE, SIDE, -1)
    return jnp.roll(field, (SHIFT_T, SHIFT_S, SHIFT_S), (0, 1, 2))


def to_heads(field_rows):
    feature_count = field_rows.shape[-1]
    windows = window_split(field_rows.reshape(FR, SIDE, SIDE, feature_count))
    return windows.reshape(NWIN, WT, feature_count // HD, HD)


def from_heads(windows):
    feature_count = windows.shape[-1] * windows.shape[-2]
    merged = window_merge(windows.reshape(NWIN, WT, feature_count))
    return merged.reshape(-1, feature_count)


def window_scores(query_win, key_win, rel_bias, keep_mask):
    scores = jnp.einsum("wihd,wjhd->whij", query_win, key_win, preferred_element_type=jnp.float32)
    scores = scores * HD ** (-0.5) + rel_bias[None]
    return jnp.where(keep_mask[:, None], scores, -1e30)


def attend_clip(query_rows, key_rows, value_rows, rel_bias, keep_mask):
    scores = window_scores(to_heads(query_rows), to_heads(key_rows), rel_bias, keep_mask)
    row_max = jnp.max(scores, axis=-1, keepdims=True)
    exponent = jnp.exp(scores - row_max)
    row_total = jnp.sum(exponent, axis=-1, keepdims=True)
    probabilities = (exponent / row_total).astype(jnp.bfloat16)
    attended = jnp.einsum(
        "whij,wjhd->wihd", probabilities, to_heads(value_rows), preferred_element_type=jnp.float32
    ).astype(jnp.bfloat16)
    return (from_heads(attended), (row_max + jnp.log(row_total))[..., 0])


def attend_back(query_rows, key_rows, value_rows, grad_rows, log_total, rel_bias, keep_mask):
    query_win = to_heads(query_rows)
    key_win = to_heads(key_rows)
    value_win = to_heads(value_rows)
    grad_win = to_heads(grad_rows)
    scores = window_scores(query_win, key_win, rel_bias, keep_mask)
    probabilities = jnp.exp(scores - log_total[..., None])
    grad_probs = jnp.einsum(
        "wihd,wjhd->whij", grad_win, value_win, preferred_element_type=jnp.float32
    )
    row_inner = jnp.sum(probabilities * grad_probs, axis=-1, keepdims=True)
    grad_scores = (probabilities * (grad_probs - row_inner)).astype(jnp.bfloat16)
    score_scale = HD ** (-0.5)
    grad_query = (
        jnp.einsum("whij,wjhd->wihd", grad_scores, key_win, preferred_element_type=jnp.float32)
        * score_scale
    )
    grad_key = (
        jnp.einsum("whij,wihd->wjhd", grad_scores, query_win, preferred_element_type=jnp.float32)
        * score_scale
    )
    grad_value = jnp.einsum(
        "whij,wihd->wjhd",
        probabilities.astype(jnp.bfloat16),
        grad_win,
        preferred_element_type=jnp.float32,
    )
    bias_term = jnp.sum(grad_scores.astype(jnp.float32), axis=0)
    return (
        from_heads(grad_query).astype(jnp.bfloat16),
        from_heads(grad_key).astype(jnp.bfloat16),
        from_heads(grad_value).astype(jnp.bfloat16),
        bias_term,
    )


def layer_pass(source, cot_block, full_weights, rel_bias, keep_mask):
    (
        norm_in_gain,
        norm_in_shift,
        qkv_w,
        qv_b,
        proj_w,
        proj_b,
        norm_mid_gain,
        norm_mid_shift,
        fc1_w,
        fc1_b,
        fc2_w,
        fc2_b,
    ) = full_weights
    clip_count = source.shape[0]
    model_width = source.shape[-1]
    shaped = (clip_count, -1, model_width)
    token_rows = source.reshape(-1, model_width).astype(jnp.float32)
    normed, norm_in_back = jax.vjp(
        layer_norm, token_rows, norm_in_gain.astype(jnp.float32), norm_in_shift.astype(jnp.float32)
    )
    normed_low = normed.astype(jnp.bfloat16)
    projected = matmul(normed_low, qkv_w)
    qv_float = qv_b.astype(jnp.float32)
    query_rows = (projected[:, :model_width] + qv_float[0]).astype(jnp.bfloat16)
    key_rows = projected[:, model_width : 2 * model_width].astype(jnp.bfloat16)
    value_rows = (projected[:, 2 * model_width :] + qv_float[1]).astype(jnp.bfloat16)
    parts = (
        lax.all_to_all(query_rows.reshape(shaped), "seq", split_axis=2, concat_axis=1, tiled=True),
        lax.all_to_all(key_rows.reshape(shaped), "seq", split_axis=2, concat_axis=1, tiled=True),
        lax.all_to_all(value_rows.reshape(shaped), "seq", split_axis=2, concat_axis=1, tiled=True),
    )
    merged_heads, log_total = lax.map(
        lambda clip_parts: attend_clip(*clip_parts, rel_bias, keep_mask), parts
    )
    attended_heads, log_total, query_heads, key_heads, value_heads = (
        merged_heads,
        log_total,
        parts[0],
        parts[1],
        parts[2],
    )
    attended = lax.all_to_all(
        attended_heads, "seq", split_axis=1, concat_axis=2, tiled=True
    ).reshape(-1, model_width)
    branch = matmul(attended, proj_w) + proj_b.astype(jnp.float32)
    middle = token_rows + branch
    normed_mid, norm_mid_back = jax.vjp(
        layer_norm, middle, norm_mid_gain.astype(jnp.float32), norm_mid_shift.astype(jnp.float32)
    )
    normed_mid_low = normed_mid.astype(jnp.bfloat16)
    hidden = matmul(normed_mid_low, fc1_w) + fc1_b.astype(jnp.float32)
    active, gelu_back = jax.vjp(gelu_exact, hidden)
    active_low = active.astype(jnp.bfloat16)
    result = matmul(active_low, fc2_w) + fc2_b.astype(jnp.float32)
    output = (middle + result).astype(jnp.bfloat16).reshape(source.shape)
    grad_low = cot_block.reshape(-1, model_width)
    grad_float = grad_low.astype(jnp.float32)
    grad_fc2_w = matmul(active_low.T, grad_low)
    grad_fc2_b = jnp.sum(grad_float, axis=0)
    grad_active = matmul(grad_low, fc2_w.T)
    grad_hidden = gelu_back(grad_active)[0].astype(jnp.bfloat16)
    grad_fc1_w = matmul(normed_mid_low.T, grad_hidden)
    grad_fc1_b = jnp.sum(grad_hidden.astype(jnp.float32), axis=0)
    grad_normed_mid = matmul(grad_hidden, fc1_w.T)
    grad_mid_part, grad_mid_gain, grad_mid_shift = norm_mid_back(grad_normed_mid)
    grad_middle = grad_float + grad_mid_part
    grad_branch = grad_middle.astype(jnp.bfloat16)
    grad_proj_w = matmul(attended.T, grad_branch)
    grad_proj_b = jnp.sum(grad_branch.astype(jnp.float32), axis=0)
    grad_attended = matmul(grad_branch, proj_w.T).astype(jnp.bfloat16)
    grad_heads = lax.all_to_all(
        grad_attended.reshape(shaped), "seq", split_axis=2, concat_axis=1, tiled=True
    )
    grad_query, grad_key, grad_value, bias_terms = lax.map(
        lambda clip_parts: attend_back(*clip_parts, rel_bias, keep_mask),
        (query_heads, key_heads, value_heads, grad_heads, log_total),
    )
    grad_query, grad_key, grad_value = (
        lax.all_to_all(grad_query, "seq", split_axis=1, concat_axis=2, tiled=True),
        lax.all_to_all(grad_key, "seq", split_axis=1, concat_axis=2, tiled=True),
        lax.all_to_all(grad_value, "seq", split_axis=1, concat_axis=2, tiled=True),
    )
    grad_query = grad_query.reshape(-1, model_width)
    grad_value = grad_value.reshape(-1, model_width)
    grad_projected = jnp.concatenate(
        [grad_query, grad_key.reshape(-1, model_width), grad_value], axis=1
    )
    grad_qkv_w = matmul(normed_low.T, grad_projected)
    grad_qv_b = jnp.stack(
        [
            jnp.sum(grad_query.astype(jnp.float32), axis=0),
            jnp.sum(grad_value.astype(jnp.float32), axis=0),
        ]
    )
    grad_normed = matmul(grad_projected, qkv_w.T)
    grad_rows_part, grad_in_gain, grad_in_shift = norm_in_back(grad_normed)
    grad_source = (grad_middle + grad_rows_part).astype(jnp.bfloat16).reshape(source.shape)
    grad_terms = (
        grad_in_gain,
        grad_in_shift,
        grad_qkv_w,
        grad_qv_b,
        grad_proj_w,
        grad_proj_b,
        grad_mid_gain,
        grad_mid_shift,
        grad_fc1_w,
        grad_fc1_b,
        grad_fc2_w,
        grad_fc2_b,
    )
    return (output, grad_source, grad_terms, jnp.sum(bias_terms, axis=0))


def shards(
    clips,
    out_grad,
    clip_order,
    region_label,
    rel_index,
    norm1_gain,
    norm1_bias,
    qkv_weight,
    qv_bias,
    bias_table,
    proj_weight,
    proj_bias,
    norm2_gain,
    norm2_bias,
    fc1_weight,
    fc1_bias,
    fc2_weight,
    fc2_bias,
):
    clip_count = clips.shape[0] // MICRO
    slot_order = clip_order[0]
    keep_mask = region_label[:, :, None] == region_label[:, None, :]
    rel_bias = jnp.take(bias_table.astype(jnp.float32), rel_index, axis=1)
    shard_set = (
        norm1_gain,
        norm1_bias,
        qkv_weight,
        qv_bias,
        proj_weight,
        proj_bias,
        norm2_gain,
        norm2_bias,
        fc1_weight,
        fc1_bias,
        fc2_weight,
        fc2_bias,
    )
    grad_sums = tuple((jnp.zeros(weight_shard.shape, jnp.float32) for weight_shard in shard_set))
    bias_sum = jnp.zeros(rel_bias.shape, jnp.float32)
    outputs = []
    source_grads = []
    for micro_index in range(MICRO):
        picked_slots = lax.dynamic_slice_in_dim(slot_order, micro_index * clip_count, clip_count)
        source = jnp.take(clips, picked_slots, axis=0)
        cot_block = out_grad[micro_index * clip_count : (micro_index + 1) * clip_count]
        full_weights = (
            lax.all_gather(norm1_gain, ("dp", "seq"), axis=0, tiled=True),
            lax.all_gather(norm1_bias, ("dp", "seq"), axis=0, tiled=True),
            lax.all_gather(qkv_weight, ("dp", "seq"), axis=0, tiled=True),
            lax.all_gather(qv_bias, ("dp", "seq"), axis=1, tiled=True),
            lax.all_gather(proj_weight, ("dp", "seq"), axis=0, tiled=True),
            lax.all_gather(proj_bias, ("dp", "seq"), axis=0, tiled=True),
            lax.all_gather(norm2_gain, ("dp", "seq"), axis=0, tiled=True),
            lax.all_gather(norm2_bias, ("dp", "seq"), axis=0, tiled=True),
            lax.all_gather(fc1_weight, ("dp", "seq"), axis=0, tiled=True),
            lax.all_gather(fc1_bias, ("dp", "seq"), axis=0, tiled=True),
            lax.all_gather(fc2_weight, ("dp", "seq"), axis=0, tiled=True),
            lax.all_gather(fc2_bias, ("dp", "seq"), axis=0, tiled=True),
        )
        output, grad_source, grad_terms, bias_term = layer_pass(
            source, cot_block, full_weights, rel_bias, keep_mask
        )
        grad_terms = (
            lax.psum_scatter(grad_terms[0], ("dp", "seq"), scatter_dimension=0, tiled=True),
            lax.psum_scatter(grad_terms[1], ("dp", "seq"), scatter_dimension=0, tiled=True),
            lax.psum_scatter(grad_terms[2], ("dp", "seq"), scatter_dimension=0, tiled=True),
            lax.psum_scatter(grad_terms[3], ("dp", "seq"), scatter_dimension=1, tiled=True),
            lax.psum_scatter(grad_terms[4], ("dp", "seq"), scatter_dimension=0, tiled=True),
            lax.psum_scatter(grad_terms[5], ("dp", "seq"), scatter_dimension=0, tiled=True),
            lax.psum_scatter(grad_terms[6], ("dp", "seq"), scatter_dimension=0, tiled=True),
            lax.psum_scatter(grad_terms[7], ("dp", "seq"), scatter_dimension=0, tiled=True),
            lax.psum_scatter(grad_terms[8], ("dp", "seq"), scatter_dimension=0, tiled=True),
            lax.psum_scatter(grad_terms[9], ("dp", "seq"), scatter_dimension=0, tiled=True),
            lax.psum_scatter(grad_terms[10], ("dp", "seq"), scatter_dimension=0, tiled=True),
            lax.psum_scatter(grad_terms[11], ("dp", "seq"), scatter_dimension=0, tiled=True),
        )
        grad_sums = tuple((previous + fresh for previous, fresh in zip(grad_sums, grad_terms)))
        bias_sum = bias_sum + bias_term
        outputs.append(output)
        source_grads.append(grad_source)
    flat_terms = bias_sum.reshape(bias_sum.shape[0], -1).T
    table_terms = jax.ops.segment_sum(flat_terms, rel_index.reshape(-1), num_segments=TBL).T
    table_grad = lax.psum(table_terms, "dp")
    output_all = jnp.concatenate(outputs, axis=0)
    clips_grad = jnp.zeros_like(clips).at[slot_order].set(jnp.concatenate(source_grads, axis=0))
    return (
        output_all,
        clips_grad,
        grad_sums[0],
        grad_sums[1],
        grad_sums[2],
        grad_sums[3],
        table_grad,
        grad_sums[4],
        grad_sums[5],
        grad_sums[6],
        grad_sums[7],
        grad_sums[8],
        grad_sums[9],
        grad_sums[10],
        grad_sums[11],
    )


EPS = 1e-5
LOG2E = math.log2(math.e)
LN2 = math.log(2.0)
SCALE = HD**-0.5
MASKED = -1e30
bf = jnp.bfloat16
f32 = jnp.float32
i32 = jnp.int32
MESH = pl.DeviceIdType.MESH
VM = pltpu.VMEM
DMA = pltpu.SemaphoreType.DMA

CL = 2
NS = 4
RP = 400
RT = CL * RP
KP = 512
C = 512
NHEAD = 16
TA = 10
TB = 256
SHARD = (16, 16, 16, 64)
WIDTH = (1536, 512, 2048, 512)
PARTS = ((0, 4), (4, 3))


def nn(a, b):
    return jnp.dot(a, b, preferred_element_type=f32)


def nt(a, b):
    return lax.dot_general(a, b, (((1,), (1,)), ((), ())), preferred_element_type=f32)


def tn(a, b):
    return lax.dot_general(a, b, (((0,), (0,)), ((), ())), preferred_element_type=f32)


def norm_parts(v):
    mu = jnp.mean(v, axis=-1, keepdims=True)
    c = v - mu
    r = lax.rsqrt(jnp.mean(c * c, axis=-1, keepdims=True) + EPS)
    return c * r, r


class Place:
    def __init__(self):
        dp, self.z = lax.axis_index("dp"), lax.axis_index("seq")
        self.dp = dp
        self.y, self.x, self.c = dp // 4, (dp // 2) % 2, dp % 2
        self.yn, self.xn, self.cn = 1 - self.y, 1 - self.x, 1 - self.c
        self.over_x = (self.dp_of(self.y, self.xn, self.c), self.z)
        self.over_y = (self.dp_of(self.yn, self.x, self.c), self.z)
        self.core = (self.dp_of(self.y, self.x, self.cn), self.z)
        self.block = dp * 4 + self.z

    def dp_of(self, y, x, c):
        return y * 4 + x * 2 + c

    def seq(self, z):
        return (self.dp, z)

    def far(self, d):
        return lax.rem(self.z + d, NS)

    def greet(self):
        bar = pltpu.get_barrier_semaphore()
        peers = [self.seq(self.far(d)) for d in (1, 2, 3)]
        peers += [self.over_x, self.over_y, self.core]
        for peer in peers:
            pl.semaphore_signal(bar, inc=1, device_id=peer, device_id_type=MESH)
        pl.semaphore_wait(bar, len(peers))


def rcopy(src, dst, ssem, rsem, dev):
    return pltpu.make_async_remote_copy(
        src_ref=src, dst_ref=dst, send_sem=ssem, recv_sem=rsem, device_id=dev, device_id_type=MESH
    )


def take(ref, sem):
    pltpu.make_async_copy(ref, ref, sem).wait()


def window_start(w, part):
    return lax.rem(7 * w + SHIFT_S + part, SIDE)


def send_windows(me, src, dst, ssem, rsem, lsem):
    slot = lax.rem(me.z + 2, NS)
    for d in range(NS):
        w = me.far(d)
        wy, wx = w // 2, lax.rem(w, 2)
        for c in range(CL):
            for y7, ny in PARTS:
                for x7, nx in PARTS:
                    a = src.at[c, pl.ds(window_start(wy, y7), ny), pl.ds(window_start(wx, x7), nx)]
                    b = dst.at[c, slot, pl.ds(y7, ny), pl.ds(x7, nx)]
                    if d == 0:
                        pltpu.make_async_copy(a, b, lsem).start()
                    else:
                        rcopy(a, b, ssem.at[d - 1], rsem.at[d - 1], me.seq(w)).start()


def take_windows(me, dst, ssem, rsem, lsem):
    for d in range(NS):
        slot = lax.rem(me.z + NS - d + 2, NS)
        if d == 0:
            take(dst.at[:, slot], lsem)
        else:
            take(dst.at[:, slot], rsem.at[d - 1])
            take(dst.at[:, slot], ssem.at[d - 1])


def send_home(me, src, dst, ssem, rsem, lsem):
    wy, wx = me.z // 2, lax.rem(me.z, 2)
    for d in range(NS):
        t = me.far(d)
        slot = lax.rem(t + 2, NS)
        for c in range(CL):
            for y7, ny in PARTS:
                for x7, nx in PARTS:
                    a = src.at[c, slot, pl.ds(y7, ny), pl.ds(x7, nx)]
                    b = dst.at[c, pl.ds(window_start(wy, y7), ny), pl.ds(window_start(wx, x7), nx)]
                    if d == 0:
                        pltpu.make_async_copy(a, b, lsem).start()
                    else:
                        rcopy(a, b, ssem.at[d - 1], rsem.at[d - 1], me.seq(t)).start()


def take_home(me, src, ssem, rsem, lsem):
    take(src.at[:, 0], lsem)
    for d in (1, 2, 3):
        take(src.at[:, 0], rsem.at[d - 1])
        take(src.at[:, 0], ssem.at[d - 1])


class Gather:
    def __init__(self, me, k, shard, full, zsem, ssem, rsem):
        self.me, self.shard, self.full, self.r = me, shard, full, SHARD[k]
        self.zsem, self.ssem, self.rsem = zsem.at[k], ssem.at[k], rsem.at[k]

    def rows(self, dp, first=0, count=NS):
        return self.full.at[pl.ds(pl.multiple_of((dp * NS + first) * self.r, self.r), count * self.r)]

    def push(self, ref, slot, dev, sem=None):
        rcopy(ref, ref, self.ssem if sem is None else sem, self.rsem.at[slot], dev).start()

    def spread(self, z):
        block = self.rows(self.me.dp, z, 1)
        self.push(block, 4 + z, self.me.over_x)
        self.push(block, 8 + z, self.me.over_y)
        self.push(block, 16 + z, self.me.core)

    def onward(self, n, act):
        z = self.me.z
        for ok, source, target in (((z >= n) & (z < NS - 1), z - n, z + 1), ((z + n < NS) & (z > 0), z + n, z - 1)):
            pl.when(ok)(functools.partial(act, self.rows(self.me.dp, source, 1), source, target))

    def along(self, n):
        self.onward(n, lambda block, source, target: self.push(block, source, self.me.seq(target), self.zsem))

    def start(self):
        me = self.me
        self.full[pl.ds(pl.multiple_of(me.block * self.r, self.r), self.r), :] = self.shard[...]
        self.along(0)
        self.spread(me.z)

    def step(self, n):
        z = self.me.z

        def came(source):
            take(self.rows(self.me.dp, source, 1), self.rsem.at[source])

        for ok, source in ((z >= n, z - n), (z + n < NS, z + n)):
            pl.when(ok)(functools.partial(came, source))
        self.along(n)
        for ok, source in ((z >= n, z - n), (z + n < NS, z + n)):
            pl.when(ok)(functools.partial(self.spread, source))

    def corner(self):
        me = self.me
        dx, dy = me.over_x[0], me.over_y[0]
        for z in range(NS):
            take(self.rows(dx, z, 1), self.rsem.at[4 + z])
            if z < 2:
                self.push(self.rows(dx, z, 1), 12 + z, me.over_y)
        self.push(self.rows(dx), 20, me.core)
        for z in range(NS):
            take(self.rows(dy, z, 1), self.rsem.at[8 + z])
            if z >= 2:
                self.push(self.rows(dy, z, 1), 12 + z, me.over_x)
        self.push(self.rows(dy), 21, me.core)

    def last(self):
        me = self.me
        dd = me.dp_of(me.yn, me.xn, me.c)
        for z in range(NS):
            take(self.rows(dd, z, 1), self.rsem.at[12 + z])
        self.push(self.rows(dd), 22, me.core)

    def finish(self):
        me = self.me
        for z in range(NS):
            take(self.rows(me.dp_of(me.y, me.x, me.cn), z, 1), self.rsem.at[16 + z])
        for slot, (y, x) in ((20, (me.y, me.xn)), (21, (me.yn, me.x)), (22, (me.yn, me.xn))):
            take(self.rows(me.dp_of(y, x, me.cn)), self.rsem.at[slot])
        for n in range(NS - 1):
            self.onward(n, lambda block, source, target: take(block, self.zsem))
        take(self.full.at[pl.ds(0, 28 * self.r)], self.ssem)


class Vectors:
    def __init__(self, me, full, ssem, rsem):
        self.me, self.full, self.ssem, self.rsem = me, full, ssem, rsem

    def rows(self, dp, first=0, count=NS):
        return self.full.at[pl.ds(dp * NS + first, count)]

    def push(self, ref, slot, dev):
        rcopy(ref, ref, self.ssem.at[slot], self.rsem.at[slot], dev).start()

    def start(self):
        me = self.me
        for d in (1, 2, 3):
            self.push(self.rows(me.dp, me.z, 1), d - 1, me.seq(me.far(d)))

    def plane(self):
        me = self.me
        for d in (1, 2, 3):
            take(self.rows(me.dp, me.far(NS - d), 1), self.rsem.at[d - 1])
        for slot, dev in ((3, me.over_x), (4, me.over_y), (5, me.core)):
            self.push(self.rows(me.dp), slot, dev)

    def diagonal(self):
        me = self.me
        dx, dy = me.over_x[0], me.over_y[0]
        take(self.rows(dx), self.rsem.at[3])
        self.push(self.rows(dx), 6, me.over_y)
        self.push(self.rows(dx), 8, me.core)
        take(self.rows(dy), self.rsem.at[4])
        self.push(self.rows(dy), 9, me.core)

    def last(self):
        me = self.me
        dd = me.dp_of(me.yn, me.xn, me.c)
        take(self.rows(dd), self.rsem.at[6])
        self.push(self.rows(dd), 10, me.core)

    def finish(self):
        me = self.me
        for slot, (y, x) in ((5, (me.y, me.x)), (8, (me.y, me.xn)), (9, (me.yn, me.x)), (10, (me.yn, me.xn))):
            take(self.rows(me.dp_of(y, x, me.cn)), self.rsem.at[slot])
        for slot in (0, 1, 2, 3, 4, 5, 6, 8, 9, 10):
            take(self.rows(0, 0, 1) if slot < 3 else self.rows(0), self.ssem.at[slot])


def pack_vectors(me, sv, g1, b1, qv, pb, g2, b2, b3, b4):
    row = jnp.zeros((1, 256), f32)
    sv[pl.ds(me.block, 1), 0] = row
    pieces = (g1[...], b1[...], qv[0:1, :], qv[1:2, :], pb[...], g2[...], b2[...], b4[...])
    for k, piece in enumerate(pieces):
        sv[pl.ds(me.block, 1), 0, 16 * k : 16 * k + 16] = piece.astype(f32)
    sv[pl.ds(me.block, 1), 0, 128:192] = b3[...].astype(f32)


def spread_vectors(sv, vec):
    v = sv[...].reshape(32, 256).astype(bf)
    lane = lax.broadcasted_iota(i32, (256, C), 1)
    row = lax.broadcasted_iota(i32, (256, C), 0)
    blk = lax.broadcasted_iota(i32, (32, C), 0)
    col = lax.broadcasted_iota(i32, (32, C), 1)
    for k in range(12):
        if k < 8:
            pick, own = row == 16 * k + (lane & 15), blk == (col >> 4)
        else:
            pick, own = row == 128 + (lane & 63), blk == (col >> 6) + 8 * (k - 8)
        y = nn(v, jnp.where(pick, 1.0, 0.0).astype(bf))
        vec[k : k + 1, :] = jnp.sum(jnp.where(own, y, 0.0), axis=0, keepdims=True)


def one_hot(lo, i):
    d = jnp.broadcast_to(lo[pl.ds(i, 1), :], (16, KP)).astype(bf)
    d = d - lax.broadcasted_iota(i32, (16, KP), 0).astype(f32).astype(bf)
    one, zero = jnp.asarray(1, bf), jnp.asarray(0, bf)
    return jnp.concatenate([jnp.where(d == jnp.asarray(16 * c, bf), one, zero) for c in range(16)], axis=0)


def order_index(me, idx, lab, perm, hi, lo, colb, lrow):
    p = perm[...]
    iv = idx[...]
    for dst, part in ((hi, iv >> 8), (lo, iv & 255)):
        rows = nn(p[0:RP, :], part.astype(f32).astype(bf)).astype(bf)
        dst[...] = nt(rows, p)
    own = lab[pl.ds(me.z, 1), :].astype(f32)
    own = jnp.broadcast_to(own, (8, WT)).astype(bf)
    lane = lax.broadcasted_iota(i32, (8, KP), 1)
    lrow[...] = jnp.where(lane < WT, nt(own, p), -1.0)
    colb[...] = jnp.broadcast_to(nt(p[0:RP, :], own)[:, 0:1], (RP, 128))


def table_rows(tbl, tab):
    whole = jnp.concatenate([tbl[s] for s in range(NS)], axis=0)
    for a in range(TA):
        tab[a * 16 : (a + 1) * 16, :] = whole[:, a * TB : (a + 1) * TB].astype(bf)


def gather_rows(first, count, tab, hi, lo, colb, lrow, bias):
    unroll = 8

    def body(t, _):
        for u in range(unroll):
            i = first + t * unroll + u
            y = nn(tab[...], one_hot(lo, i))
            high = jnp.broadcast_to(hi[pl.ds(i, 1), :], (16, KP))
            acc = jnp.zeros((16, KP), f32)
            for a in range(TA):
                acc = jnp.where(high == a, y[a * 16 : (a + 1) * 16], acc)
            acc = acc * LOG2E
            own = colb[pl.ds(i, 1), :]
            r0 = pl.multiple_of(i * 16, 16)
            for j in range(4):
                keep = lrow[0:1, j * 128 : (j + 1) * 128] == own
                bias[j, pl.ds(r0, 16), :] = jnp.where(keep, acc[:, j * 128 : (j + 1) * 128], MASKED)
        return 0

    lax.fori_loop(0, count // unroll, body, 0)


def scatter_rows(first, count, g, other, hi, lo, total):
    unroll = 8
    zero = jnp.asarray(0, bf)

    def body(t, _):
        ls, rs = [], []
        for u in range(unroll):
            n = t * unroll + u
            i = first + n
            rs.append(one_hot(lo, i))
            high = jnp.broadcast_to(hi[pl.ds(i, 1), :], (16, KP)).astype(bf)
            r0 = pl.multiple_of(i * 16, 16)
            own = jnp.concatenate([g[j, pl.ds(r0, 16), :] for j in range(4)], axis=1)
            own = (own + other[pl.ds(pl.multiple_of(n * 16, 16), 16), :].astype(f32)).astype(bf)
            ls.append(
                jnp.concatenate([jnp.where(high == jnp.asarray(a, bf), own, zero) for a in range(TA)], axis=0)
            )
        total[...] += nt(jnp.concatenate(ls, axis=1), jnp.concatenate(rs, axis=1))
        return 0

    lax.fori_loop(0, count // unroll, body, 0)


def load_tokens(src, clip, dst, p):
    for s in range(NS):
        v = src[clip, s].astype(f32).reshape(98, C)
        dst[p * RP + s * 98 : p * RP + (s + 1) * 98, :] = v.astype(dst.dtype)
    dst[p * RP + WT : (p + 1) * RP, :] = jnp.zeros((RP - WT, C), dst.dtype)


def store_tokens(src, clip, dst, slot):
    for s in range(NS):
        v = src[clip, s * 98 : (s + 1) * 98, :]
        dst[slot, s] = v.reshape(49, 2, C).astype(bf).reshape(7, 7, 2, C)


def qkv_phase(x, vec, wq, n1, q, k, v):
    for p in range(CL):
        k[p, RP:KP, :] = jnp.zeros((KP - RP, C), bf)
        v[p, RP:KP, :] = jnp.zeros((KP - RP, C), bf)

    def body(p, _):
        r0 = pl.multiple_of(p * RP, RP)
        n, _r = norm_parts(x[pl.ds(r0, RP), :].astype(f32))
        y = (n * vec[0:1, :] + vec[1:2, :]).astype(bf)
        n1[pl.ds(r0, RP), :] = y
        q[pl.ds(r0, RP), :] = ((nn(y, wq[:, 0:C]) + vec[2:3, :]) * (SCALE * LOG2E)).astype(bf)
        k[p, 0:RP, :] = nn(y, wq[:, C : 2 * C]).astype(bf)
        v[p, 0:RP, :] = (nn(y, wq[:, 2 * C : 3 * C]) + vec[3:4, :]).astype(bf)
        return 0

    lax.fori_loop(0, CL, body, 0)


def attention_forward(q, k, v, bias, e, att, inv, poll):
    lane = lax.broadcasted_iota(i32, (1, 128), 1) // HD

    def body(t, _):
        quad, p = t // CL, lax.rem(t, CL)
        l0 = pl.multiple_of(quad * 128, 128)
        r = pl.ds(pl.multiple_of(p * RP, RP), RP)
        qq = q[r, pl.ds(l0, 128)]
        kk = k[p, :, pl.ds(l0, 128)]
        vv = v[p, :, pl.ds(l0, 128)]
        acc = jnp.zeros((RP, 128), f32)
        ainv = acc
        for hq in range(4):
            h = quad * 4 + hq
            s = nt(qq, jnp.where(lane == hq, kk, jnp.zeros_like(kk)))
            s = s + jnp.concatenate([bias[j, pl.ds(h, RP, stride=16), :] for j in range(4)], axis=1)
            w = jnp.exp2(s - jnp.max(s, axis=1, keepdims=True)).astype(bf)
            e[p, h] = w
            o = nn(w, jnp.where(lane == hq, vv, jnp.ones_like(vv)))
            one = 1.0 / pltpu.roll(o, HD, 1)
            acc = jnp.where(lane == hq, o * one, acc)
            ainv = jnp.where(lane == hq, one, ainv)
        att[r, pl.ds(l0, 128)] = acc.astype(bf)
        inv[r, pl.ds(l0, 128)] = ainv
        poll(t)
        return 0

    lax.fori_loop(0, 4 * CL, body, 0)


def feed_forward(x, dy, att, vec, wp, w1, w2, nm, mid, acc, out, gvec):
    for p in range(CL):
        r = slice(p * RP, (p + 1) * RP)
        m = x[r, :].astype(f32) + nn(att[r, :], wp[...]) + vec[4:5, :]
        mid[r, :] = m
        n, _ = norm_parts(m)
        nm[r, :] = (n * vec[5:6, :] + vec[6:7, :]).astype(bf)
        out[p] = m + vec[7:8, :]
    acc[...] = jnp.zeros_like(acc)
    gvec[7:8, :] = jnp.sum(dy[...].astype(f32), axis=0, keepdims=True)

    def body(c, _):
        c0 = pl.multiple_of(c * C, C)
        g1 = g2 = gb = None
        for p in range(CL):
            r = slice(p * RP, (p + 1) * RP)
            hid = nn(nm[r, :], w1[:, pl.ds(c0, C)]) + vec[pl.ds(8 + c, 1), :]
            density = jnp.exp2(hid * hid * (-0.5 * LOG2E)) * (1 / math.sqrt(2 * math.pi))
            phi = 0.5 * (1.0 + lax.erf(hid * (1 / math.sqrt(2.0))))
            act = (hid * phi).astype(bf)
            slope = phi + hid * density
            out[p] += nn(act, w2[pl.ds(c0, C), :])
            dh = (nt(dy[r, :], w2[pl.ds(c0, C), :]) * slope).astype(bf)
            acc[r, :] += nt(dh, w1[:, pl.ds(c0, C)])
            a2, a1, ab = tn(act, dy[r, :]), tn(nm[r, :], dh), jnp.sum(dh.astype(f32), axis=0, keepdims=True)
            g2, g1, gb = (a2, a1, ab) if p == 0 else (g2 + a2, g1 + a1, gb + ab)
        gvec[pl.ds(8 + c, 1), :] = gb
        w2[pl.ds(c0, C), :] = g2.astype(bf)
        w1[:, pl.ds(c0, C)] = g1.astype(bf)
        return 0

    lax.fori_loop(0, 4, body, 0)


def middle_backward(dy, att, vec, wp, mid, acc, inv, gvec, do):
    s4 = s5 = s6 = jnp.zeros((1, C), f32)
    parts = []
    for p in range(CL):
        r = slice(p * RP, (p + 1) * RP)
        n, rr = norm_parts(mid[r, :])
        gmn = acc[r, :]
        s5 += jnp.sum(gmn * n, axis=0, keepdims=True)
        s6 += jnp.sum(gmn, axis=0, keepdims=True)
        g = gmn * vec[5:6, :]
        gm = dy[r, :].astype(f32) + rr * (
            g - jnp.mean(g, axis=-1, keepdims=True) - n * jnp.mean(g * n, axis=-1, keepdims=True)
        )
        mid[r, :] = gm
        gb = gm.astype(bf)
        s4 += jnp.sum(gb.astype(f32), axis=0, keepdims=True)
        parts.append(gb)
        low = (nt(gb, wp[...]) * inv[r, :]).astype(bf)
        do[r, :] = low
        acc[r, :] = low.astype(f32) * att[r, :].astype(f32)
    gvec[4:5, :] = s4
    gvec[5:6, :] = s5
    gvec[6:7, :] = s6
    wp[...] = tn(att[...], jnp.concatenate(parts, axis=0)).astype(bf)


def attention_backward(q, k, v, e, do, prod, g, dq, dk, dv, poll):
    lane = lax.broadcasted_iota(i32, (1, 128), 1) // HD

    def body(quad, _):
        l0 = pl.multiple_of(quad * 128, 128)
        dqs = [jnp.zeros((RP, 128), f32) for _ in range(CL)]
        dks, dvs = [[], []], [[], []]
        qts = [q[p * RP : (p + 1) * RP, pl.ds(l0, 128)].T for p in range(CL)]
        dots = [do[p * RP : (p + 1) * RP, pl.ds(l0, 128)].T for p in range(CL)]
        for hq in range(4):
            h = quad * 4 + hq
            f = slice(hq * HD, (hq + 1) * HD)
            both = None
            for p in range(CL):
                r = slice(p * RP, (p + 1) * RP)
                kk = k[p, :, pl.ds(l0, 128)]
                vv = v[p, :, pl.ds(l0, 128)]
                dp = nt(do[r, pl.ds(l0, 128)], jnp.where(lane == hq, vv, jnp.zeros_like(vv)))
                inner = jnp.sum(jnp.where(lane == hq, prod[r, pl.ds(l0, 128)], 0.0), axis=1, keepdims=True)
                w = e[p, h]
                ds = w.astype(f32) * (dp - inner)
                both = ds if both is None else both + ds
                low = ds.astype(bf)
                dqs[p] = dqs[p] + nn(low, jnp.where(lane == hq, kk, jnp.zeros_like(kk)))
                dks[p].append((nn(qts[p][f], low) * LN2).astype(bf))
                dvs[p].append(nn(dots[p][f], w).astype(bf))
            for j in range(4):
                g[j, pl.ds(h, RP, stride=16), :] = both[:, j * 128 : (j + 1) * 128]
            if hq == 1:
                poll(quad, 0)
        for p in range(CL):
            r = slice(p * RP, (p + 1) * RP)
            dq[r, pl.ds(l0, 128)] = (dqs[p] * SCALE).astype(bf)
            dk[r, pl.ds(l0, 128)] = jnp.concatenate(dks[p], axis=0).T[0:RP]
            dv[p, 0:RP, pl.ds(l0, 128)] = jnp.concatenate(dvs[p], axis=0).T[0:RP]
        poll(quad, 1)
        return 0

    lax.fori_loop(0, 4, body, 0)


def input_backward(x, n1, vec, wq, dq, dk, dv, mid, dx, gvec):
    s0 = s1 = s3 = jnp.zeros((1, C), f32)
    gvec[2:3, :] = jnp.sum(dq[...].astype(f32), axis=0, keepdims=True)
    for p in range(CL):
        r = slice(p * RP, (p + 1) * RP)
        dvp = dv[p, 0:RP, :]
        s3 += jnp.sum(dvp.astype(f32), axis=0, keepdims=True)
        gn = nt(dq[r, :], wq[:, 0:C]) + nt(dk[r, :], wq[:, C : 2 * C]) + nt(dvp, wq[:, 2 * C : 3 * C])
        n, rr = norm_parts(x[r, :].astype(f32))
        s0 += jnp.sum(gn * n, axis=0, keepdims=True)
        s1 += jnp.sum(gn, axis=0, keepdims=True)
        g = gn * vec[0:1, :]
        dx[p] = mid[r, :] + rr * (
            g - jnp.mean(g, axis=-1, keepdims=True) - n * jnp.mean(g * n, axis=-1, keepdims=True)
        )
    gvec[0:1, :] = s0
    gvec[1:2, :] = s1
    gvec[3:4, :] = s3
    n1t = n1[...].T
    wq[:, 0:C] = nn(n1t, dq[...]).astype(bf)
    wq[:, C : 2 * C] = nn(n1t, dk[...]).astype(bf)
    dva = jnp.concatenate([dv[p, 0:RP, :] for p in range(CL)], axis=0)
    wq[:, 2 * C : 3 * C] = nn(n1t, dva).astype(bf)


class Reduce:
    def __init__(self, me, k, grad, out, ssem, rsem, rc, rx, ry, ra, rz):
        self.me, self.r, self.grad, self.out = me, SHARD[k], grad, out
        self.u = 4 * self.r
        self.h = self.u // 2
        self.ssem, self.rsem = ssem.at[k], rsem.at[k]
        self.rc, self.rx, self.ry, self.ra, self.rz = rc, rx, ry, ra, rz

    def own(self, y, x, c, first=0, count=None):
        return pl.ds(pl.multiple_of(self.me.dp_of(y, x, c) * self.u + first, self.r), self.u if count is None else count)

    def send(self, rows, dst, slot, dev):
        rcopy(self.grad.at[rows], dst, self.ssem.at[slot], self.rsem.at[slot], dev).start()

    def add(self, rows, part, slot):
        take(part, self.rsem.at[slot])
        self.grad[rows, :] = (self.grad[rows, :].astype(f32) + part[...].astype(f32)).astype(bf)

    def cores(self):
        me = self.me
        for g in range(4):
            self.send(self.own(g // 2, g % 2, me.cn), self.rc.at[g], g, me.core)

    def plane(self):
        me, h = self.me, self.h
        for g in range(4):
            self.add(self.own(g // 2, g % 2, me.c), self.rc.at[g], g)
        for n in range(2):
            self.send(self.own(n, me.xn, me.c, 0, h), self.rx.at[n], 4 + n, me.over_x)
            self.send(self.own(me.yn, n, me.c, h, h), self.ry.at[n], 6 + n, me.over_y)

    def corner(self):
        me, h = self.me, self.h
        for n in range(2):
            self.add(self.own(n, me.x, me.c, 0, h), self.rx.at[n], 4 + n)
            self.add(self.own(me.y, n, me.c, h, h), self.ry.at[n], 6 + n)
        self.send(self.own(me.yn, me.x, me.c, 0, h), self.ra.at[0], 8, me.over_y)
        self.send(self.own(me.y, me.xn, me.c, h, h), self.ra.at[1], 9, me.over_x)

    def line(self):
        me, h, r = self.me, self.h, self.r
        for n in range(2):
            self.add(self.own(me.y, me.x, me.c, n * h, h), self.ra.at[n], 8 + n)
        for d in (1, 2, 3):
            z = me.far(d)
            self.send(self.own(me.y, me.x, me.c, z * r, r), self.rz.at[d - 1], 9 + d, me.seq(z))

    def finish(self):
        me, r, u, h = self.me, self.r, self.u, self.h
        total = self.grad[self.own(me.y, me.x, me.c, me.z * r, r), :].astype(f32)
        for d in (1, 2, 3):
            take(self.rz.at[d - 1], self.rsem.at[9 + d])
            total = total + self.rz[d - 1].astype(f32)
        self.out[...] = total
        for slot in range(13):
            count = u if slot < 4 else h if slot < 10 else r
            take(self.grad.at[pl.ds(0, count)], self.ssem.at[slot])


SEG = 40
SEGS = RP // 2 // SEG


def block_kernel(
    order, clips, cot, sq, sp, s1, s2, g1, b1, qv, pb, g2, b2, b3, b4, table, lab, idx, perm,
    out_t, dx_t, oq, op, o1, o2, og1, ob1, oqv, opb, og2, ob2, ob3, ob4, otab,
    bg, e, wq, wp, w1, w2, xw, dyw, x, dy, n1, q, k, v, att, inv, nm, mid, acc, out, do,
    hi, lo, sv, tbl, tab, colb, lrow, vec, gvec, total, tz, tx, vz, vx,
    *rest,
):
    parts = [rest[5 * n : 5 * n + 5] for n in range(4)]
    (xs, xr, xl, ds_, dr, dl, os_, or_, ol, hs, hr, hl, wz, ws, wr, vs, vr, ts, tr, bs, br, free, es, er,
     rs, rr, zs, zr, as_, ar) = rest[20:]
    me = Place()
    me.greet()
    pack_vectors(me, sv, g1, b1, qv, pb, g2, b2, b3, b4)
    tbl[pl.ds(me.z, 1), :, 2432:2560] = jnp.zeros((1, 4, 128), f32)
    tbl[pl.ds(me.z, 1), :, 0:TBL] = table[...].astype(f32)[None]
    weights = [
        Gather(me, n, shard, full, wz, ws, wr)
        for n, (shard, full) in enumerate(((sq, wq), (sp, wp), (s1, w1), (s2, w2)))
    ]
    later = [weights[1], weights[2], weights[3]]
    vectors = Vectors(me, sv, vs, vr)
    for d in (1, 2, 3):
        own = tbl.at[me.z]
        rcopy(own, own, ts.at[d - 1], tr.at[d - 1], me.seq(me.far(d))).start()
    vectors.start()
    weights[0].start()
    send_windows(me, clips, xw, xs, xr, xl)
    order_index(me, idx, lab, perm, hi, lo, colb, lrow)
    weights[0].step(1)
    for d in (1, 2, 3):
        take(tbl.at[0], tr.at[d - 1])
        take(tbl.at[0], ts.at[d - 1])
    table_rows(tbl, tab)

    def bias_rows(n, half):
        return bg.at[:, pl.ds(pl.multiple_of((half * SEGS + n) * SEG * 16, 16), SEG * 16)]

    def rows(n):
        gather_rows((me.c * SEGS + n) * SEG, SEG, tab, hi, lo, colb, lrow, bg)
        part = bias_rows(n, me.c)
        rcopy(part, part, bs.at[n], br.at[n], me.core).start()

    weights[0].step(2)
    vectors.plane()
    rows(0)
    weights[0].step(3)
    rows(1)
    vectors.diagonal()
    weights[0].corner()
    rows(2)
    vectors.last()
    weights[0].last()
    rows(3)
    vectors.finish()
    spread_vectors(sv, vec)
    for w in later:
        w.start()
    rows(4)
    weights[0].finish()
    take_windows(me, xw, xs, xr, xl)
    send_windows(me, cot, dyw, ds_, dr, dl)
    for p in range(CL):
        load_tokens(xw, p, x, p)
    for w in later:
        w.step(1)
    qkv_phase(x, vec, wq, n1, q, k, v)
    for n in range(SEGS):
        take(bias_rows(n, me.cn), br.at[n])
        take(bias_rows(n, me.c), bs.at[n])

    def forward_poll(t):
        steps = {0: lambda w: w.step(2), 1: lambda w: w.step(3), 3: lambda w: w.corner(), 5: lambda w: w.last()}
        for at, step in steps.items():

            def go(step=step):
                for w in later:
                    step(w)

            pl.when(t == at)(go)

    attention_forward(q, k, v, bg, e, att, inv, forward_poll)
    gvec[...] = jnp.zeros_like(gvec)
    for w in later:
        w.finish()
    take_windows(me, dyw, ds_, dr, dl)
    for p in range(CL):
        load_tokens(dyw, order[0, p], dy, p)
    feed_forward(x, dy, att, vec, wp, w1, w2, nm, mid, acc, out, gvec)
    reds = [
        Reduce(me, n, grad, total_out, rs, rr, *parts[n])
        for n, (grad, total_out) in enumerate(((wq, oq), (wp, op), (w1, o1), (w2, o2)))
    ]
    reds[2].cores()
    reds[3].cores()
    for p in range(CL):
        store_tokens(out, order[0, p], xw, p)
    send_home(me, xw, out_t, os_, or_, ol)
    middle_backward(dy, att, vec, wp, mid, acc, inv, gvec, do)
    reds[1].cores()
    reds[2].plane()

    def backward_poll(quad, half):
        def go1():
            reds[3].plane()
            reds[1].plane()

        def go2():
            reds[2].corner()

        if half == 0:
            pl.when(quad == 1)(go1)
        else:
            pl.when(quad == 3)(go2)

    attention_backward(q, k, v, e, do, acc, bg, nm, att, v, backward_poll)
    pl.semaphore_signal(free, inc=1, device_id=me.core, device_id_type=MESH)
    input_backward(x, n1, vec, wq, nm, att, v, mid, out, gvec)
    reds[0].cores()
    for p in range(CL):
        store_tokens(out, p, dyw, p)
    send_home(me, dyw, dx_t, hs, hr, hl)
    for d in (1, 2, 3):
        rcopy(gvec, vz.at[d - 1], zs.at[d - 1], zr.at[d - 1], me.seq(me.far(d))).start()
    other, halves = SEG * 16, ((0, 384), (1, 256))
    for n in range(SEGS):
        r0 = pl.multiple_of((me.cn * SEGS + n) * other, 16)
        lowered = jnp.concatenate([bg[j, pl.ds(r0, other), :] for j in range(4)], axis=1).astype(bf)
        e[1, 2 * n, 0:384, :] = lowered[0:384]
        e[1, 2 * n + 1, 0:256, :] = lowered[384:640]
        if n == 0:
            pl.semaphore_wait(free, 1)
        for m, count in halves:
            rcopy(
                e.at[1, 2 * n + m, pl.ds(0, count)], e.at[0, 2 * n + m, pl.ds(0, count)],
                es.at[2 * n + m], er.at[2 * n + m], me.core,
            ).start()
    total[...] = jnp.zeros_like(total)

    def scatter(n):
        for m, count in halves:
            take(e.at[0, 2 * n + m, pl.ds(0, count)], er.at[2 * n + m])
        first = (me.c * SEGS + n) * SEG
        scatter_rows(first, 24, bg, e.at[0, 2 * n], hi, lo, total)
        scatter_rows(first + 24, 16, bg, e.at[0, 2 * n + 1], hi, lo, total)

    scatter(0)
    reds[0].plane()
    reds[3].corner()
    reds[1].corner()
    scatter(1)
    reds[2].line()
    scatter(2)
    reds[0].corner()
    reds[3].line()
    reds[1].line()
    vecs = gvec[...]
    for d in (1, 2, 3):
        take(vz.at[d - 1], zr.at[d - 1])
        vecs = vecs + vz[d - 1]
    scatter(3)
    reds[0].line()
    scatter(4)
    for a in range(TA):
        for s in range(NS):
            tbl[s, :, a * TB : (a + 1) * TB] = total[a * 16 + 4 * s : a * 16 + 4 * s + 4, :]
    for d in (1, 2, 3):
        rcopy(tbl.at[me.far(d)], tz.at[d - 1], zs.at[2 + d], zr.at[2 + d], me.seq(me.far(d))).start()
    table = tbl[pl.ds(me.z, 1)].reshape(4, TA * TB)
    for n in (2, 3, 1):
        reds[n].finish()
    for d in (1, 2, 3):
        take(tz.at[d - 1], zr.at[2 + d])
        table = table + tz[d - 1]
    for n, dev in enumerate((me.core, me.over_x, me.over_y)):
        tx[2 * n] = table
        vx[2 * n] = vecs
        rcopy(tx.at[2 * n], tx.at[2 * n + 1], as_.at[2 * n], ar.at[2 * n], dev).start()
        rcopy(vx.at[2 * n], vx.at[2 * n + 1], as_.at[2 * n + 1], ar.at[2 * n + 1], dev).start()
        take(tx.at[2 * n + 1], ar.at[2 * n])
        take(vx.at[2 * n + 1], ar.at[2 * n + 1])
        table = table + tx[2 * n + 1]
        vecs = vecs + vx[2 * n + 1]
    otab[...] = table
    vx[6] = vecs
    part = pltpu.roll(vecs[0:8, :], C - me.block * 16, 1)
    for row, ref in ((0, og1), (1, ob1), (4, opb), (5, og2), (6, ob2), (7, ob4)):
        ref[...] = part[row : row + 1, 0:16]
    oqv[...] = part[2:4, 0:16]
    wide = jnp.broadcast_to(vx[6, pl.ds(8 + me.block // 8, 1), :], (8, C))
    ob3[...] = pltpu.roll(wide, C - lax.rem(me.block, 8) * 64, 1)[0:1, 0:64]
    reds[0].finish()
    for n in range(SEGS):
        for m, count in halves:
            take(e.at[1, 2 * n + m, pl.ds(0, count)], es.at[2 * n + m])
    for n in range(3):
        take(tx.at[0], as_.at[2 * n])
        take(vx.at[0], as_.at[2 * n + 1])
        take(vz.at[0], zs.at[n])
        take(tz.at[0], zs.at[3 + n])
    take_home(me, xw, os_, or_, ol)
    take_home(me, dyw, hs, hr, hl)


def publish_kernel(*refs):
    n = len(refs) // 2
    for source, target in zip(refs[:n], refs[n:]):
        target[...] = source[...]


def windowed(
    clips, out_grad, clip_order, region_label, rel_index, norm1_gain, norm1_bias, qkv_weight, qv_bias,
    bias_table, proj_weight, proj_bias, norm2_gain, norm2_bias, fc1_weight, fc1_bias, fc2_weight, fc2_bias,
):
    at = np.arange(WT)
    canonical = (2 * (at // 98) + at % 2) * 49 + (at % 98) // 2
    perm = np.zeros((KP, WT), np.float32)
    perm[at, canonical] = 1
    perm = jnp.asarray(perm, bf)
    field = lambda a: jnp.transpose(a, (0, 2, 3, 1, 4))
    row = lambda a: a.reshape(1, -1)
    spec = lambda space: pl.BlockSpec(memory_space=space)
    win = (CL, NS, 7, 7, 2, C)
    whole = ((C, 1536), (C, C), (C, 2048), (2048, C))
    rows = (RT, C)
    keys = (CL, KP, C)
    tab = (4, TA * TB)
    reduce_scratch = []
    for r, w in zip(SHARD, WIDTH):
        u, h = 4 * r, 2 * r
        reduce_scratch += [VM((n, m, w), bf) for n, m in ((4, u), (2, h), (2, h), (2, h), (3, r))]
    field_shape = (CL, SIDE, SIDE, 2, C)
    outs = [
        (field_shape, bf), (field_shape, bf), *(((r, w), f32) for r, w in zip(SHARD, WIDTH)),
        ((1, 16), f32), ((1, 16), f32), ((2, 16), f32), ((1, 16), f32), ((1, 16), f32), ((1, 16), f32), ((1, 64), f32),
        ((1, 16), f32), (tab, f32),
    ]
    outs = [jax.ShapeDtypeStruct(s, d) for s, d in outs]
    results = pl.pallas_call(
        block_kernel,
        out_shape=outs,
        in_specs=[spec(pltpu.SMEM)] + [spec(pl.ANY)] * 2 + [spec(VM)] * 16,
        out_specs=[spec(pl.ANY)] * 2 + [spec(VM)] * 13,
        scratch_shapes=[
            VM((4, RP * 16, 128), f32), VM((CL, NHEAD, RP, KP), bf), *(VM(s, bf) for s in whole), VM(win, bf), VM(win, bf),
            VM(rows, bf), VM(rows, bf), VM(rows, bf), VM(rows, bf), VM(keys, bf), VM(keys, bf),
            VM(rows, bf), VM(rows, f32), VM(rows, bf), VM(rows, f32), VM(rows, f32), VM((CL, RP, C), f32), VM(rows, bf),
            VM((RP, KP), f32), VM((RP, KP), f32), VM((32, 1, 256), f32), VM((NS, *tab), f32), VM((TA * 16, TB), bf),
            VM((RP, 128), f32), VM((8, KP), f32), VM((16, C), f32), VM((16, C), f32), VM((TA * 16, TB), f32),
            VM((3, *tab), f32), VM((6, *tab), f32), VM((3, 16, C), f32), VM((7, 16, C), f32),
            *reduce_scratch,
            *(DMA((3,)), DMA((3,)), DMA) * 4,
            DMA((4,)), DMA((4,)), DMA((4, 23)), DMA((11,)), DMA((11,)), DMA((3,)), DMA((3,)),
            DMA((SEGS,)), DMA((SEGS,)), pltpu.SemaphoreType.REGULAR, DMA((2 * SEGS,)), DMA((2 * SEGS,)),
            DMA((4, 13)), DMA((4, 13)), DMA((6,)), DMA((6,)), DMA((6,)), DMA((6,)),
        ],
        compiler_params=pltpu.CompilerParams(
            collective_id=0, has_side_effects=True, vmem_limit_bytes=64 * 1024 * 1024 - 64 * 1024
        ),
    )(
        clip_order, field(clips), field(out_grad), qkv_weight, proj_weight, fc1_weight, fc2_weight,
        row(norm1_gain), row(norm1_bias), qv_bias, row(proj_bias), row(norm2_gain), row(norm2_bias),
        row(fc1_bias), row(fc2_bias), bias_table, region_label, rel_index, perm,
    )
    out_t, dx_t, oq, op, o1, o2, og1, ob1, oqv, opb, og2, ob2, ob3, ob4, otab = pl.pallas_call(
        publish_kernel,
        out_shape=outs,
        in_specs=[spec(VM)] * 15,
        out_specs=[spec(VM)] * 15,
    )(*results)
    back = lambda a: jnp.transpose(a, (0, 3, 1, 2, 4))
    flat = lambda a: a.reshape(-1)
    return (
        back(out_t), back(dx_t), flat(og1), flat(ob1), oq, oqv, otab[:, :TBL], op, flat(opb), flat(og2), flat(ob2),
        o1, flat(ob3), o2, flat(ob4),
    )


def solution(mesh):
    in_specs = (
        P("dp", "seq", None, None, None),
        P("dp", "seq", None, None, None),
        P("dp", None),
        P(),
        P(),
        P(("dp", "seq")),
        P(("dp", "seq")),
        P(("dp", "seq"), None),
        P(None, ("dp", "seq")),
        P("seq", None),
        P(("dp", "seq"), None),
        P(("dp", "seq")),
        P(("dp", "seq")),
        P(("dp", "seq")),
        P(("dp", "seq"), None),
        P(("dp", "seq")),
        P(("dp", "seq"), None),
        P(("dp", "seq")),
    )
    out_specs = (
        P("dp", "seq", None, None, None),
        P("dp", "seq", None, None, None),
        P(("dp", "seq")),
        P(("dp", "seq")),
        P(("dp", "seq"), None),
        P(None, ("dp", "seq")),
        P("seq", None),
        P(("dp", "seq"), None),
        P(("dp", "seq")),
        P(("dp", "seq")),
        P(("dp", "seq")),
        P(("dp", "seq"), None),
        P(("dp", "seq")),
        P(("dp", "seq"), None),
        P(("dp", "seq")),
    )
    local = windowed if mesh.shape["dp"] == 8 and mesh.shape["seq"] == NS else shards
    return jax.shard_map(local, mesh=mesh, in_specs=in_specs, out_specs=out_specs, check_vma=False)
```

profile of v0, /device:TPU:0, one launch (start us, length us, event | category | flops | bytes accessed | tf_op | source)
XLA Modules:
  0.0 189.5 jit_solution(14942198609859213827)
XLA Ops:
  0.7 185.8 %shard_map.298 = (bf16[2,14,14,2,512]{4,3,2,1,0:T(2,128)(2,1)}, bf16[2,14,14,2,512]{4,3,2,1,0:T(2,128)(2,1)}, f32[16,1536]{1,0:T(8,128)}, f32[16,512]{1,0:T(8,12...) custom-call(s32[1,2]{1,0:T(1,128)} %order.1, ...), custom_call_target="tpu_custom_call" | custom-call | tf_op jit(solution)/shard_map/pallas_call | solution.py:1181
  186.4 2.9 %shard_map.299 = (bf16[2,14,14,2,512]{4,3,2,1,0:T(2,128)(2,1)}, bf16[2,14,14,2,512]{4,3,2,1,0:T(2,128)(2,1)}, f32[16,1536]{1,0:T(8,128)}, f32[16,512]{1,0:T(8,12...) custom-call(bf16[2,14,14,2,512]{4,3,2,1,0:T(2,128)(2,1)} %get-tuple-, ...), custom_call_target="tpu_custom_call" | custom-call | tf_op jit(solution)/shard_map/pallas_call | solution.py:1207
where the time goes:
time: 190 us
  Pallas kernels  189 us (99%)
    pallas_call x1, Pallas kernels, windowed(): pl.pallas_call(block_kernel, out_shape=outs, in_specs=[spec(pltpu.SMEM)]...  186 us

commit v1 on v0

--- a/solution.py
+++ b/solution.py
@@ -359,6 +359,7 @@
 C = 512
 NHEAD = 16
 TA = 10
+HR = 17
 TB = 256
 SHARD = (16, 16, 16, 64)
 WIDTH = (1536, 512, 2048, 512)
@@ -393,7 +394,11 @@
         self.over_x = (self.dp_of(self.y, self.xn, self.c), self.z)
         self.over_y = (self.dp_of(self.yn, self.x, self.c), self.z)
         self.core = (self.dp_of(self.y, self.x, self.cn), self.z)
+        self.corner = (self.dp_of(self.yn, self.xn, self.c), self.z)
         self.block = dp * 4 + self.z
+        self.z1 = self.z + 1 - 2 * lax.rem(self.z, 2)
+        self.z2 = lax.rem(self.z + 2, NS)
+        self.z3 = NS - 1 - self.z
 
     def dp_of(self, y, x, c):
         return y * 4 + x * 2 + c
@@ -406,11 +411,13 @@
 
     def greet(self):
         bar = pltpu.get_barrier_semaphore()
-        peers = [self.seq(self.far(d)) for d in (1, 2, 3)]
-        peers += [self.over_x, self.over_y, self.core]
-        for peer in peers:
+        self.peers = [self.seq(self.far(d)) for d in (1, 2, 3)]
+        self.peers += [self.over_x, self.over_y, self.corner, self.core]
+        for peer in self.peers:
             pl.semaphore_signal(bar, inc=1, device_id=peer, device_id_type=MESH)
-        pl.semaphore_wait(bar, len(peers))
+
+    def met(self):
+        pl.semaphore_wait(pltpu.get_barrier_semaphore(), len(self.peers))
 
 
 def rcopy(src, dst, ssem, rsem, dev):
@@ -427,30 +434,29 @@
     return lax.rem(7 * w + SHIFT_S + part, SIDE)
 
 
-def send_windows(me, src, dst, ssem, rsem, lsem):
+def send_windows(me, c, src, dst, ssem, rsem, lsem):
     slot = lax.rem(me.z + 2, NS)
     for d in range(NS):
         w = me.far(d)
         wy, wx = w // 2, lax.rem(w, 2)
-        for c in range(CL):
-            for y7, ny in PARTS:
-                for x7, nx in PARTS:
-                    a = src.at[c, pl.ds(window_start(wy, y7), ny), pl.ds(window_start(wx, x7), nx)]
-                    b = dst.at[c, slot, pl.ds(y7, ny), pl.ds(x7, nx)]
-                    if d == 0:
-                        pltpu.make_async_copy(a, b, lsem).start()
-                    else:
-                        rcopy(a, b, ssem.at[d - 1], rsem.at[d - 1], me.seq(w)).start()
-
-
-def take_windows(me, dst, ssem, rsem, lsem):
+        for y7, ny in PARTS:
+            for x7, nx in PARTS:
+                a = src.at[c, pl.ds(window_start(wy, y7), ny), pl.ds(window_start(wx, x7), nx)]
+                b = dst.at[c, slot, pl.ds(y7, ny), pl.ds(x7, nx)]
+                if d == 0:
+                    pltpu.make_async_copy(a, b, lsem.at[c]).start()
+                else:
+                    rcopy(a, b, ssem.at[c, d - 1], rsem.at[c, d - 1], me.seq(w)).start()
+
+
+def take_windows(me, c, dst, ssem, rsem, lsem):
     for d in range(NS):
-        slot = lax.rem(me.z + NS - d + 2, NS)
+        part = dst.at[c, lax.rem(me.z + NS - d + 2, NS)]
         if d == 0:
-            take(dst.at[:, slot], lsem)
+            take(part, lsem.at[c])
         else:
-            take(dst.at[:, slot], rsem.at[d - 1])
-            take(dst.at[:, slot], ssem.at[d - 1])
+            take(part, rsem.at[c, d - 1])
+            take(part, ssem.at[c, d - 1])
 
 
 def send_home(me, src, dst, ssem, rsem, lsem):
@@ -493,31 +499,28 @@
         self.push(block, 8 + z, self.me.over_y)
         self.push(block, 16 + z, self.me.core)
 
-    def onward(self, n, act):
-        z = self.me.z
-        for ok, source, target in (((z >= n) & (z < NS - 1), z - n, z + 1), ((z + n < NS) & (z > 0), z + n, z - 1)):
-            pl.when(ok)(functools.partial(act, self.rows(self.me.dp, source, 1), source, target))
-
-    def along(self, n):
-        self.onward(n, lambda block, source, target: self.push(block, source, self.me.seq(target), self.zsem))
+    def fill(self):
+        self.full[pl.ds(pl.multiple_of(self.me.block * self.r, self.r), self.r), :] = self.shard[...]
 
     def start(self):
         me = self.me
-        self.full[pl.ds(pl.multiple_of(me.block * self.r, self.r), self.r), :] = self.shard[...]
-        self.along(0)
         self.spread(me.z)
-
-    def step(self, n):
-        z = self.me.z
-
-        def came(source):
-            take(self.rows(self.me.dp, source, 1), self.rsem.at[source])
-
-        for ok, source in ((z >= n, z - n), (z + n < NS, z + n)):
-            pl.when(ok)(functools.partial(came, source))
-        self.along(n)
-        for ok, source in ((z >= n, z - n), (z + n < NS, z + n)):
-            pl.when(ok)(functools.partial(self.spread, source))
+        for z in (me.z2, me.z1):
+            self.push(self.rows(me.dp, me.z, 1), me.z, me.seq(z), self.zsem)
+
+    def came(self, z):
+        take(self.rows(self.me.dp, z, 1), self.rsem.at[z])
+
+    def step1(self):
+        me = self.me
+        self.came(me.z2)
+        self.push(self.rows(me.dp, me.z2, 1), me.z2, me.seq(me.z1), self.zsem)
+        self.spread(me.z2)
+
+    def step2(self):
+        for z in (self.me.z1, self.me.z3):
+            self.came(z)
+            self.spread(z)
 
     def corner(self):
         me = self.me
@@ -546,9 +549,21 @@
             take(self.rows(me.dp_of(me.y, me.x, me.cn), z, 1), self.rsem.at[16 + z])
         for slot, (y, x) in ((20, (me.y, me.xn)), (21, (me.yn, me.x)), (22, (me.yn, me.xn))):
             take(self.rows(me.dp_of(y, x, me.cn)), self.rsem.at[slot])
-        for n in range(NS - 1):
-            self.onward(n, lambda block, source, target: take(block, self.zsem))
+        take(self.full.at[pl.ds(0, 3 * self.r)], self.zsem)
         take(self.full.at[pl.ds(0, 28 * self.r)], self.ssem)
+
+
+class DirectGather(Gather):
+    def spread(self, z):
+        super().spread(z)
+        self.push(self.rows(self.me.dp, z, 1), 12 + z, self.me.corner)
+
+    def groups(self):
+        me = self.me
+        for n, device in enumerate((me.over_x, me.over_y, me.corner)):
+            for z in range(NS):
+                take(self.rows(device[0], z, 1), self.rsem.at[(4, 8, 12)[n] + z])
+            self.push(self.rows(device[0]), 20 + n, me.core)
 
 
 class Vectors:
@@ -641,13 +656,13 @@
 
 
 def table_rows(tbl, tab):
-    whole = jnp.concatenate([tbl[s] for s in range(NS)], axis=0)
+    whole = jnp.concatenate([tbl[s].astype(f32) for s in range(NS)], axis=0)
     for a in range(TA):
         tab[a * 16 : (a + 1) * 16, :] = whole[:, a * TB : (a + 1) * TB].astype(bf)
 
 
 def gather_rows(first, count, tab, hi, lo, colb, lrow, bias):
-    unroll = 8
+    unroll = 20
 
     def body(t, _):
         for u in range(unroll):
@@ -659,7 +674,7 @@
                 acc = jnp.where(high == a, y[a * 16 : (a + 1) * 16], acc)
             acc = acc * LOG2E
             own = colb[pl.ds(i, 1), :]
-            r0 = pl.multiple_of(i * 16, 16)
+            r0 = i * HR
             for j in range(4):
                 keep = lrow[0:1, j * 128 : (j + 1) * 128] == own
                 bias[j, pl.ds(r0, 16), :] = jnp.where(keep, acc[:, j * 128 : (j + 1) * 128], MASKED)
@@ -669,7 +684,7 @@
 
 
 def scatter_rows(first, count, g, other, hi, lo, total):
-    unroll = 8
+    unroll = 10
     zero = jnp.asarray(0, bf)
 
     def body(t, _):
@@ -679,13 +694,10 @@
             i = first + n
             rs.append(one_hot(lo, i))
             high = jnp.broadcast_to(hi[pl.ds(i, 1), :], (16, KP)).astype(bf)
-            r0 = pl.multiple_of(i * 16, 16)
-            own = jnp.concatenate([g[j, pl.ds(r0, 16), :] for j in range(4)], axis=1)
+            own = jnp.concatenate([g[j, pl.ds(i * HR, 16), :] for j in range(4)], axis=1)
             own = (own + other[pl.ds(pl.multiple_of(n * 16, 16), 16), :].astype(f32)).astype(bf)
-            ls.append(
-                jnp.concatenate([jnp.where(high == jnp.asarray(a, bf), own, zero) for a in range(TA)], axis=0)
-            )
-        total[...] += nt(jnp.concatenate(ls, axis=1), jnp.concatenate(rs, axis=1))
+            ls.append(jnp.concatenate([jnp.where(high == jnp.asarray(a, bf), own, zero) for a in range(TA)], axis=0))
+        total[...] += nt(jnp.concatenate(rs, axis=1), jnp.concatenate(ls, axis=1))
         return 0
 
     lax.fori_loop(0, count // unroll, body, 0)
@@ -704,55 +716,47 @@
         dst[slot, s] = v.reshape(49, 2, C).astype(bf).reshape(7, 7, 2, C)
 
 
-def qkv_phase(x, vec, wq, n1, q, k, v):
-    for p in range(CL):
-        k[p, RP:KP, :] = jnp.zeros((KP - RP, C), bf)
-        v[p, RP:KP, :] = jnp.zeros((KP - RP, C), bf)
-
-    def body(p, _):
-        r0 = pl.multiple_of(p * RP, RP)
-        n, _r = norm_parts(x[pl.ds(r0, RP), :].astype(f32))
-        y = (n * vec[0:1, :] + vec[1:2, :]).astype(bf)
-        n1[pl.ds(r0, RP), :] = y
-        q[pl.ds(r0, RP), :] = ((nn(y, wq[:, 0:C]) + vec[2:3, :]) * (SCALE * LOG2E)).astype(bf)
-        k[p, 0:RP, :] = nn(y, wq[:, C : 2 * C]).astype(bf)
-        v[p, 0:RP, :] = (nn(y, wq[:, 2 * C : 3 * C]) + vec[3:4, :]).astype(bf)
-        return 0
-
-    lax.fori_loop(0, CL, body, 0)
-
-
-def attention_forward(q, k, v, bias, e, att, inv, poll):
+def qkv_phase(p, x, vec, wq, n1, q, k, v):
+    r = slice(p * RP, (p + 1) * RP)
+    k[p, RP:KP, :] = jnp.zeros((KP - RP, C), bf)
+    v[p, RP:KP, :] = jnp.zeros((KP - RP, C), bf)
+    n, _ = norm_parts(x[r, :].astype(f32))
+    y = (n * vec[0:1, :] + vec[1:2, :]).astype(bf)
+    n1[r, :] = y
+    q[r, :] = ((nn(y, wq[:, 0:C]) + vec[2:3, :]) * (SCALE * LOG2E)).astype(bf)
+    k[p, 0:RP, :] = nn(y, wq[:, C : 2 * C]).astype(bf)
+    v[p, 0:RP, :] = (nn(y, wq[:, 2 * C : 3 * C]) + vec[3:4, :]).astype(bf)
+
+
+def attention_forward(p, q, k, v, bias, e, att, inv, poll):
     lane = lax.broadcasted_iota(i32, (1, 128), 1) // HD
 
-    def body(t, _):
-        quad, p = t // CL, lax.rem(t, CL)
+    def body(quad, _):
         l0 = pl.multiple_of(quad * 128, 128)
-        r = pl.ds(pl.multiple_of(p * RP, RP), RP)
+        r = slice(p * RP, (p + 1) * RP)
         qq = q[r, pl.ds(l0, 128)]
         kk = k[p, :, pl.ds(l0, 128)]
         vv = v[p, :, pl.ds(l0, 128)]
-        acc = jnp.zeros((RP, 128), f32)
-        ainv = acc
+        acc = sums = jnp.zeros((RP, 128), f32)
         for hq in range(4):
             h = quad * 4 + hq
             s = nt(qq, jnp.where(lane == hq, kk, jnp.zeros_like(kk)))
-            s = s + jnp.concatenate([bias[j, pl.ds(h, RP, stride=16), :] for j in range(4)], axis=1)
+            s = s + jnp.concatenate([bias[j, pl.ds(h, RP, stride=HR), :] for j in range(4)], axis=1)
             w = jnp.exp2(s - jnp.max(s, axis=1, keepdims=True)).astype(bf)
             e[p, h] = w
             o = nn(w, jnp.where(lane == hq, vv, jnp.ones_like(vv)))
-            one = 1.0 / pltpu.roll(o, HD, 1)
-            acc = jnp.where(lane == hq, o * one, acc)
-            ainv = jnp.where(lane == hq, one, ainv)
-        att[r, pl.ds(l0, 128)] = acc.astype(bf)
+            acc = jnp.where(lane == hq, o, acc)
+            sums = jnp.where(lane == (hq + 1) % 4, o, sums)
+        ainv = 1.0 / pltpu.roll(sums, 128 - HD, 1)
+        att[r, pl.ds(l0, 128)] = (acc * ainv).astype(bf)
         inv[r, pl.ds(l0, 128)] = ainv
-        poll(t)
+        poll(quad)
         return 0
 
-    lax.fori_loop(0, 4 * CL, body, 0)
-
-
-def feed_forward(x, dy, att, vec, wp, w1, w2, nm, mid, acc, out, gvec):
+    lax.fori_loop(0, 4, body, 0)
+
+
+def feed_forward(x, att, vec, wp, w1, w2, nm, mid, out, keep):
     for p in range(CL):
         r = slice(p * RP, (p + 1) * RP)
         m = x[r, :].astype(f32) + nn(att[r, :], wp[...]) + vec[4:5, :]
@@ -760,12 +764,9 @@
         n, _ = norm_parts(m)
         nm[r, :] = (n * vec[5:6, :] + vec[6:7, :]).astype(bf)
         out[p] = m + vec[7:8, :]
-    acc[...] = jnp.zeros_like(acc)
-    gvec[7:8, :] = jnp.sum(dy[...].astype(f32), axis=0, keepdims=True)
 
     def body(c, _):
         c0 = pl.multiple_of(c * C, C)
-        g1 = g2 = gb = None
         for p in range(CL):
             r = slice(p * RP, (p + 1) * RP)
             hid = nn(nm[r, :], w1[:, pl.ds(c0, C)]) + vec[pl.ds(8 + c, 1), :]
@@ -774,13 +775,39 @@
             act = (hid * phi).astype(bf)
             slope = phi + hid * density
             out[p] += nn(act, w2[pl.ds(c0, C), :])
-            dh = (nt(dy[r, :], w2[pl.ds(c0, C), :]) * slope).astype(bf)
-            acc[r, :] += nt(dh, w1[:, pl.ds(c0, C)])
+            for j in range(4):
+                t = slice(j * 128, (j + 1) * 128)
+                keep[c, j * RT + p * RP : j * RT + (p + 1) * RP, :] = slope[:, t]
+                keep[c, (4 + j) * RT + p * RP : (4 + j) * RT + (p + 1) * RP, :] = act[:, t].astype(f32)
+        return 0
+
+    lax.fori_loop(0, 4, body, 0)
+
+
+def feed_backward(dy, w1, w2, nm, acc, gvec, keep, poll):
+    acc[...] = jnp.zeros_like(acc)
+    gvec[7:8, :] = jnp.sum(dy[...].astype(f32), axis=0, keepdims=True)
+
+    def body(c, _):
+        c0 = pl.multiple_of(c * C, C)
+        g1 = g2 = gb = None
+        for p in range(CL):
+            r = slice(p * RP, (p + 1) * RP)
+
+            def kept(n):
+                return jnp.concatenate(
+                    [keep[c, (n + j) * RT + p * RP : (n + j) * RT + (p + 1) * RP, :] for j in range(4)], axis=1
+                )
+
+            dh = (nt(dy[r, :], w2[pl.ds(c0, C), :]) * kept(0)).astype(bf)
+            acc[p] += nt(dh, w1[:, pl.ds(c0, C)])
+            act = kept(4).astype(bf)
             a2, a1, ab = tn(act, dy[r, :]), tn(nm[r, :], dh), jnp.sum(dh.astype(f32), axis=0, keepdims=True)
             g2, g1, gb = (a2, a1, ab) if p == 0 else (g2 + a2, g1 + a1, gb + ab)
         gvec[pl.ds(8 + c, 1), :] = gb
         w2[pl.ds(c0, C), :] = g2.astype(bf)
         w1[:, pl.ds(c0, C)] = g1.astype(bf)
+        poll(c)
         return 0
 
     lax.fori_loop(0, 4, body, 0)
@@ -792,7 +819,7 @@
     for p in range(CL):
         r = slice(p * RP, (p + 1) * RP)
         n, rr = norm_parts(mid[r, :])
-        gmn = acc[r, :]
+        gmn = acc[p]
         s5 += jnp.sum(gmn * n, axis=0, keepdims=True)
         s6 += jnp.sum(gmn, axis=0, keepdims=True)
         g = gmn * vec[5:6, :]
@@ -805,7 +832,7 @@
         parts.append(gb)
         low = (nt(gb, wp[...]) * inv[r, :]).astype(bf)
         do[r, :] = low
-        acc[r, :] = low.astype(f32) * att[r, :].astype(f32)
+        acc[p] = low.astype(f32) * att[r, :].astype(f32)
     gvec[4:5, :] = s4
     gvec[5:6, :] = s5
     gvec[6:7, :] = s6
@@ -830,7 +857,7 @@
                 kk = k[p, :, pl.ds(l0, 128)]
                 vv = v[p, :, pl.ds(l0, 128)]
                 dp = nt(do[r, pl.ds(l0, 128)], jnp.where(lane == hq, vv, jnp.zeros_like(vv)))
-                inner = jnp.sum(jnp.where(lane == hq, prod[r, pl.ds(l0, 128)], 0.0), axis=1, keepdims=True)
+                inner = jnp.sum(jnp.where(lane == hq, prod[p, :, pl.ds(l0, 128)], 0.0), axis=1, keepdims=True)
                 w = e[p, h]
                 ds = w.astype(f32) * (dp - inner)
                 both = ds if both is None else both + ds
@@ -839,7 +866,7 @@
                 dks[p].append((nn(qts[p][f], low) * LN2).astype(bf))
                 dvs[p].append(nn(dots[p][f], w).astype(bf))
             for j in range(4):
-                g[j, pl.ds(h, RP, stride=16), :] = both[:, j * 128 : (j + 1) * 128]
+                g[j, pl.ds(h, RP, stride=HR), :] = both[:, j * 128 : (j + 1) * 128]
             if hq == 1:
                 poll(quad, 0)
         for p in range(CL):
@@ -894,12 +921,14 @@
 
     def add(self, rows, part, slot):
         take(part, self.rsem.at[slot])
-        self.grad[rows, :] = (self.grad[rows, :].astype(f32) + part[...].astype(f32)).astype(bf)
+        self.grad[rows, :] = self.grad[rows, :] + part[...]
+
+    def core_part(self, g):
+        self.send(self.own(g // 2, g % 2, self.me.cn), self.rc.at[g], g, self.me.core)
 
     def cores(self):
-        me = self.me
         for g in range(4):
-            self.send(self.own(g // 2, g % 2, me.cn), self.rc.at[g], g, me.core)
+            self.core_part(g)
 
     def plane(self):
         me, h = self.me, self.h
@@ -909,6 +938,20 @@
             self.send(self.own(n, me.xn, me.c, 0, h), self.rx.at[n], 4 + n, me.over_x)
             self.send(self.own(me.yn, n, me.c, h, h), self.ry.at[n], 6 + n, me.over_y)
 
+    def plane_part(self, g):
+        me, h = self.me, self.h
+        y, x = g // 2, g % 2
+        self.add(self.own(y, x, me.c), self.rc.at[g], g)
+
+        def over_x():
+            self.send(self.own(y, x, me.c, 0, h), self.rx.at[y], 4 + y, me.over_x)
+
+        def over_y():
+            self.send(self.own(y, x, me.c, h, h), self.ry.at[x], 6 + x, me.over_y)
+
+        pl.when(x == me.xn)(over_x)
+        pl.when(y == me.yn)(over_y)
+
     def corner(self):
         me, h = self.me, self.h
         for n in range(2):
@@ -921,16 +964,21 @@
         me, h, r = self.me, self.h, self.r
         for n in range(2):
             self.add(self.own(me.y, me.x, me.c, n * h, h), self.ra.at[n], 8 + n)
-        for d in (1, 2, 3):
-            z = me.far(d)
-            self.send(self.own(me.y, me.x, me.c, z * r, r), self.rz.at[d - 1], 9 + d, me.seq(z))
+        for n, z in enumerate((me.z1, me.z3)):
+            self.send(self.own(me.y, me.x, me.c, z * r, r), self.rz.at[n], 10 + n, me.seq(me.z1))
+
+    def across(self):
+        me, r = self.me, self.r
+        rows = self.own(me.y, me.x, me.c, me.z2 * r, r)
+        self.add(rows, self.rz.at[1], 11)
+        self.send(rows, self.rz.at[2], 12, me.seq(me.z2))
 
     def finish(self):
         me, r, u, h = self.me, self.r, self.u, self.h
         total = self.grad[self.own(me.y, me.x, me.c, me.z * r, r), :].astype(f32)
-        for d in (1, 2, 3):
-            take(self.rz.at[d - 1], self.rsem.at[9 + d])
-            total = total + self.rz[d - 1].astype(f32)
+        for n, slot in ((0, 10), (2, 12)):
+            take(self.rz.at[n], self.rsem.at[slot])
+            total = total + self.rz[n].astype(f32)
         self.out[...] = total
         for slot in range(13):
             count = u if slot < 4 else h if slot < 10 else r
@@ -944,8 +992,8 @@
 def block_kernel(
     order, clips, cot, sq, sp, s1, s2, g1, b1, qv, pb, g2, b2, b3, b4, table, lab, idx, perm,
     out_t, dx_t, oq, op, o1, o2, og1, ob1, oqv, opb, og2, ob2, ob3, ob4, otab,
-    bg, e, wq, wp, w1, w2, xw, dyw, x, dy, n1, q, k, v, att, inv, nm, mid, acc, out, do,
-    hi, lo, sv, tbl, tab, colb, lrow, vec, gvec, total, tz, tx, vz, vx,
+    bg, e, wq, wp, w1, w2, xw, dyw, x, dy, n1, q, k, v, att, inv, nm, mid, out, do,
+    hi, lo, sv, tbl, tblb, tab, colb, lrow, vec, gvec, total, tz, tx, vz, vx,
     *rest,
 ):
     parts = [rest[5 * n : 5 * n + 5] for n in range(4)]
@@ -953,123 +1001,152 @@
      rs, rr, zs, zr, as_, ar) = rest[20:]
     me = Place()
     me.greet()
+    weights = [
+        kind(me, n, shard, full, wz, ws, wr)
+        for n, (kind, shard, full) in enumerate(
+            ((DirectGather, sq, wq), (Gather, sp, wp), (Gather, s1, w1), (Gather, s2, w2))
+        )
+    ]
+    first, later = weights[0], weights[1:]
+    for w in weights:
+        w.fill()
     pack_vectors(me, sv, g1, b1, qv, pb, g2, b2, b3, b4)
-    tbl[pl.ds(me.z, 1), :, 2432:2560] = jnp.zeros((1, 4, 128), f32)
-    tbl[pl.ds(me.z, 1), :, 0:TBL] = table[...].astype(f32)[None]
-    weights = [
-        Gather(me, n, shard, full, wz, ws, wr)
-        for n, (shard, full) in enumerate(((sq, wq), (sp, wp), (s1, w1), (s2, w2)))
-    ]
-    later = [weights[1], weights[2], weights[3]]
+    tblb[pl.ds(me.z, 1), :, 2432:2560] = jnp.zeros((1, 4, 128), bf)
+    tblb[pl.ds(me.z, 1), :, 0:TBL] = table[...][None]
     vectors = Vectors(me, sv, vs, vr)
+    order_index(me, idx, lab, perm, hi, lo, colb, lrow)
+    me.met()
     for d in (1, 2, 3):
-        own = tbl.at[me.z]
+        own = tblb.at[me.z]
         rcopy(own, own, ts.at[d - 1], tr.at[d - 1], me.seq(me.far(d))).start()
+    first.start()
     vectors.start()
-    weights[0].start()
-    send_windows(me, clips, xw, xs, xr, xl)
-    order_index(me, idx, lab, perm, hi, lo, colb, lrow)
-    weights[0].step(1)
+    send_windows(me, 0, clips, xw, xs, xr, xl)
+    for w in later:
+        w.start()
     for d in (1, 2, 3):
-        take(tbl.at[0], tr.at[d - 1])
-        take(tbl.at[0], ts.at[d - 1])
-    table_rows(tbl, tab)
+        take(tblb.at[0], tr.at[d - 1])
+        take(tblb.at[0], ts.at[d - 1])
+    table_rows(tblb, tab)
 
     def bias_rows(n, half):
-        return bg.at[:, pl.ds(pl.multiple_of((half * SEGS + n) * SEG * 16, 16), SEG * 16)]
+        return bg.at[:, pl.ds(pl.multiple_of((half * SEGS + n) * SEG * HR, 8), SEG * HR)]
 
     def rows(n):
         gather_rows((me.c * SEGS + n) * SEG, SEG, tab, hi, lo, colb, lrow, bg)
         part = bias_rows(n, me.c)
         rcopy(part, part, bs.at[n], br.at[n], me.core).start()
 
-    weights[0].step(2)
+    rows(0)
+    first.step1()
+    first.step2()
     vectors.plane()
-    rows(0)
-    weights[0].step(3)
     rows(1)
     vectors.diagonal()
-    weights[0].corner()
     rows(2)
+    first.groups()
     vectors.last()
-    weights[0].last()
     rows(3)
     vectors.finish()
     spread_vectors(sv, vec)
-    for w in later:
-        w.start()
     rows(4)
-    weights[0].finish()
-    take_windows(me, xw, xs, xr, xl)
-    send_windows(me, cot, dyw, ds_, dr, dl)
-    for p in range(CL):
+    first.finish()
+
+    def first_poll(quad):
+        def second():
+            for w in later:
+                w.step2()
+
+        pl.when(quad == 2)(second)
+
+    def second_poll(quad):
+        def last():
+            for w in later:
+                w.last()
+
+        pl.when(quad == 1)(last)
+
+    for p, poll in enumerate((first_poll, second_poll)):
+        if p == 1:
+            for w in later:
+                w.corner()
+        take_windows(me, p, xw, xs, xr, xl)
+        if p == 0:
+            for w in later:
+                w.step1()
+            send_windows(me, 1, clips, xw, xs, xr, xl)
+            for c in range(CL):
+                send_windows(me, c, cot, dyw, ds_, dr, dl)
         load_tokens(xw, p, x, p)
-    for w in later:
-        w.step(1)
-    qkv_phase(x, vec, wq, n1, q, k, v)
-    for n in range(SEGS):
-        take(bias_rows(n, me.cn), br.at[n])
-        take(bias_rows(n, me.c), bs.at[n])
-
-    def forward_poll(t):
-        steps = {0: lambda w: w.step(2), 1: lambda w: w.step(3), 3: lambda w: w.corner(), 5: lambda w: w.last()}
-        for at, step in steps.items():
-
-            def go(step=step):
-                for w in later:
-                    step(w)
-
-            pl.when(t == at)(go)
-
-    attention_forward(q, k, v, bg, e, att, inv, forward_poll)
+        qkv_phase(p, x, vec, wq, n1, q, k, v)
+        if p == 0:
+            for n in range(SEGS):
+                take(bias_rows(n, me.cn), br.at[n])
+                take(bias_rows(n, me.c), bs.at[n])
+        attention_forward(p, q, k, v, bg, e, att, inv, poll)
     gvec[...] = jnp.zeros_like(gvec)
     for w in later:
         w.finish()
-    take_windows(me, dyw, ds_, dr, dl)
+    feed_forward(x, att, vec, wp, w1, w2, nm, mid, out, bg)
     for p in range(CL):
-        load_tokens(dyw, order[0, p], dy, p)
-    feed_forward(x, dy, att, vec, wp, w1, w2, nm, mid, acc, out, gvec)
+        store_tokens(out, order[0, p], xw, p)
+    send_home(me, xw, out_t, os_, or_, ol)
     reds = [
         Reduce(me, n, grad, total_out, rs, rr, *parts[n])
         for n, (grad, total_out) in enumerate(((wq, oq), (wp, op), (w1, o1), (w2, o2)))
     ]
+    for p in range(CL):
+        take_windows(me, p, dyw, ds_, dr, dl)
+    for p in range(CL):
+        load_tokens(dyw, order[0, p], dy, p)
+
+    def chunk_poll(c):
+        reds[3].core_part(c)
+        pl.when(c > 0)(lambda: reds[3].plane_part(c - 1))
+
+    feed_backward(dy, w1, w2, nm, out, gvec, bg, chunk_poll)
     reds[2].cores()
-    reds[3].cores()
-    for p in range(CL):
-        store_tokens(out, order[0, p], xw, p)
-    send_home(me, xw, out_t, os_, or_, ol)
-    middle_backward(dy, att, vec, wp, mid, acc, inv, gvec, do)
+    reds[3].plane_part(3)
+    middle_backward(dy, att, vec, wp, mid, out, inv, gvec, do)
     reds[1].cores()
+    reds[3].corner()
     reds[2].plane()
 
     def backward_poll(quad, half):
-        def go1():
-            reds[3].plane()
-            reds[1].plane()
-
-        def go2():
-            reds[2].corner()
-
-        if half == 0:
-            pl.when(quad == 1)(go1)
-        else:
-            pl.when(quad == 3)(go2)
-
-    attention_backward(q, k, v, e, do, acc, bg, nm, att, v, backward_poll)
+        def both(name):
+            for n in (2, 1):
+                getattr(reds[n], name)()
+
+        steps = ((0, reds[1].plane), (2, reds[3].line), (4, reds[3].across))
+        steps += ((5, lambda: both("corner")), (7, lambda: both("line")))
+        for n, step in steps:
+            if half == n % 2:
+                pl.when(quad == n // 2)(step)
+
+    attention_backward(q, k, v, e, do, out, bg, nm, att, v, backward_poll)
     pl.semaphore_signal(free, inc=1, device_id=me.core, device_id_type=MESH)
     input_backward(x, n1, vec, wq, nm, att, v, mid, out, gvec)
     reds[0].cores()
+    for d in (1, 2, 3):
+        rcopy(gvec, vz.at[d - 1], zs.at[d - 1], zr.at[d - 1], me.seq(me.far(d))).start()
+    for n in (2, 1):
+        reds[n].across()
     for p in range(CL):
         store_tokens(out, p, dyw, p)
     send_home(me, dyw, dx_t, hs, hr, hl)
-    for d in (1, 2, 3):
-        rcopy(gvec, vz.at[d - 1], zs.at[d - 1], zr.at[d - 1], me.seq(me.far(d))).start()
-    other, halves = SEG * 16, ((0, 384), (1, 256))
+    halves = ((0, SEG * 8), (1, SEG * 8))
     for n in range(SEGS):
-        r0 = pl.multiple_of((me.cn * SEGS + n) * other, 16)
-        lowered = jnp.concatenate([bg[j, pl.ds(r0, other), :] for j in range(4)], axis=1).astype(bf)
-        e[1, 2 * n, 0:384, :] = lowered[0:384]
-        e[1, 2 * n + 1, 0:256, :] = lowered[384:640]
+
+        def lower(i, _, n=n):
+            for m in range(2):
+                for u in range(2):
+                    at = m * SEG // 2 + u * SEG // 4 + i
+                    r0 = ((me.cn * SEGS + n) * SEG + at) * HR
+                    row = jnp.concatenate([bg[j, pl.ds(r0, 16), :] for j in range(4)], axis=1)
+                    e[1, 2 * n + m, pl.ds(pl.multiple_of((u * SEG // 4 + i) * 16, 16), 16), :] = row.astype(bf)
+            return 0
+
+        lax.fori_loop(0, SEG // 4, lower, 0)
         if n == 0:
             pl.semaphore_wait(free, 1)
         for m, count in halves:
@@ -1083,37 +1160,35 @@
         for m, count in halves:
             take(e.at[0, 2 * n + m, pl.ds(0, count)], er.at[2 * n + m])
         first = (me.c * SEGS + n) * SEG
-        scatter_rows(first, 24, bg, e.at[0, 2 * n], hi, lo, total)
-        scatter_rows(first + 24, 16, bg, e.at[0, 2 * n + 1], hi, lo, total)
+        for m in range(2):
+            scatter_rows(first + m * SEG // 2, SEG // 2, bg, e.at[0, 2 * n + m], hi, lo, total)
 
     scatter(0)
     reds[0].plane()
-    reds[3].corner()
-    reds[1].corner()
     scatter(1)
-    reds[2].line()
     scatter(2)
     reds[0].corner()
-    reds[3].line()
-    reds[1].line()
+    scatter(3)
+    reds[0].line()
+    scatter(4)
+    sums = total[...].T
+    for a in range(TA):
+        for s in range(NS):
+            tbl[s, :, a * TB : (a + 1) * TB] = sums[a * 16 + 4 * s : a * 16 + 4 * s + 4, :]
+    tblb[...] = tbl[...].astype(bf)
+    for d in (1, 2, 3):
+        rcopy(tblb.at[me.far(d)], tz.at[d - 1], zs.at[2 + d], zr.at[2 + d], me.seq(me.far(d))).start()
+    reds[0].across()
+    table = tbl[pl.ds(me.z, 1)].reshape(4, TA * TB)
     vecs = gvec[...]
     for d in (1, 2, 3):
         take(vz.at[d - 1], zr.at[d - 1])
         vecs = vecs + vz[d - 1]
-    scatter(3)
-    reds[0].line()
-    scatter(4)
-    for a in range(TA):
-        for s in range(NS):
-            tbl[s, :, a * TB : (a + 1) * TB] = total[a * 16 + 4 * s : a * 16 + 4 * s + 4, :]
-    for d in (1, 2, 3):
-        rcopy(tbl.at[me.far(d)], tz.at[d - 1], zs.at[2 + d], zr.at[2 + d], me.seq(me.far(d))).start()
-    table = tbl[pl.ds(me.z, 1)].reshape(4, TA * TB)
     for n in (2, 3, 1):
         reds[n].finish()
     for d in (1, 2, 3):
         take(tz.at[d - 1], zr.at[2 + d])
-        table = table + tz[d - 1]
+        table = table + tz[d - 1].astype(f32)
     for n, dev in enumerate((me.core, me.over_x, me.over_y)):
         tx[2 * n] = table
         vx[2 * n] = vecs
@@ -1184,14 +1259,14 @@
         in_specs=[spec(pltpu.SMEM)] + [spec(pl.ANY)] * 2 + [spec(VM)] * 16,
         out_specs=[spec(pl.ANY)] * 2 + [spec(VM)] * 13,
         scratch_shapes=[
-            VM((4, RP * 16, 128), f32), VM((CL, NHEAD, RP, KP), bf), *(VM(s, bf) for s in whole), VM(win, bf), VM(win, bf),
+            VM((4, RP * HR, 128), f32), VM((CL, NHEAD, RP, KP), bf), *(VM(s, bf) for s in whole), VM(win, bf), VM(win, bf),
             VM(rows, bf), VM(rows, bf), VM(rows, bf), VM(rows, bf), VM(keys, bf), VM(keys, bf),
-            VM(rows, bf), VM(rows, f32), VM(rows, bf), VM(rows, f32), VM(rows, f32), VM((CL, RP, C), f32), VM(rows, bf),
-            VM((RP, KP), f32), VM((RP, KP), f32), VM((32, 1, 256), f32), VM((NS, *tab), f32), VM((TA * 16, TB), bf),
-            VM((RP, 128), f32), VM((8, KP), f32), VM((16, C), f32), VM((16, C), f32), VM((TA * 16, TB), f32),
-            VM((3, *tab), f32), VM((6, *tab), f32), VM((3, 16, C), f32), VM((7, 16, C), f32),
+            VM(rows, bf), VM(rows, f32), VM(rows, bf), VM(rows, f32), VM((CL, RP, C), f32), VM(rows, bf),
+            VM((RP, KP), f32), VM((RP, KP), f32), VM((32, 1, 256), f32), VM((NS, *tab), f32), VM((NS, *tab), bf), VM((TA * 16, TB), bf),
+            VM((RP, 128), f32), VM((8, KP), f32), VM((16, C), f32), VM((16, C), f32), VM((TB, TA * 16), f32),
+            VM((3, *tab), bf), VM((6, *tab), f32), VM((3, 16, C), f32), VM((7, 16, C), f32),
             *reduce_scratch,
-            *(DMA((3,)), DMA((3,)), DMA) * 4,
+            *(DMA((2, 3)), DMA((2, 3)), DMA((2,))) * 2, *(DMA((3,)), DMA((3,)), DMA) * 2,
             DMA((4,)), DMA((4,)), DMA((4, 23)), DMA((11,)), DMA((11,)), DMA((3,)), DMA((3,)),
             DMA((SEGS,)), DMA((SEGS,)), pltpu.SemaphoreType.REGULAR, DMA((2 * SEGS,)), DMA((2 * SEGS,)),
             DMA((4, 13)), DMA((4, 13)), DMA((6,)), DMA((6,)), DMA((6,)), DMA((6,)),

time: 190 us -> 151 us (0.79)
  Pallas kernels: 189 us -> 149 us
    pallas_call x1, Pallas kernels: 186 us -> 147 us  [windowed(): pl.pallas_call(block_kernel, out_shape=outs, in_specs=[spec(pltpu.SMEM)]...]
where the time goes in v1:
time: 151 us; the launch traced here: 150 us
  Pallas kernels  149 us (99%)
    pallas_call x1, Pallas kernels, windowed(): pl.pallas_call(block_kernel, out_shape=outs, in_specs=[spec(pltpu.SMEM)]...  147 us

profile of v1, /device:TPU:0, one launch (start us, length us, event | category | flops | bytes accessed | tf_op | source)
XLA Modules:
  0.0 150.3 jit_solution(3277843918455479037)
XLA Ops:
  0.7 146.5 %shard_map.298 = (bf16[2,14,14,2,512]{4,3,2,1,0:T(2,128)(2,1)}, bf16[2,14,14,2,512]{4,3,2,1,0:T(2,128)(2,1)}, f32[16,1536]{1,0:T(8,128)}, f32[16,512]{1,0:T(8,12...) custom-call(s32[1,2]{1,0:T(1,128)} %order.1, ...), custom_call_target="tpu_custom_call" | custom-call | tf_op jit(solution)/shard_map/pallas_call | solution.py:1256
  147.2 2.9 %shard_map.299 = (bf16[2,14,14,2,512]{4,3,2,1,0:T(2,128)(2,1)}, bf16[2,14,14,2,512]{4,3,2,1,0:T(2,128)(2,1)}, f32[16,1536]{1,0:T(8,128)}, f32[16,512]{1,0:T(8,12...) custom-call(bf16[2,14,14,2,512]{4,3,2,1,0:T(2,128)(2,1)} %get-tuple-, ...), custom_call_target="tpu_custom_call" | custom-call | tf_op jit(solution)/shard_map/pallas_call | solution.py:1282

commit v2 on v1

--- a/solution.py
+++ b/solution.py
@@ -459,12 +459,12 @@
             take(part, ssem.at[c, d - 1])
 
 
-def send_home(me, src, dst, ssem, rsem, lsem):
+def send_home(me, clips, src, dst, ssem, rsem, lsem):
     wy, wx = me.z // 2, lax.rem(me.z, 2)
     for d in range(NS):
         t = me.far(d)
         slot = lax.rem(t + 2, NS)
-        for c in range(CL):
+        for c in clips:
             for y7, ny in PARTS:
                 for x7, nx in PARTS:
                     a = src.at[c, slot, pl.ds(y7, ny), pl.ds(x7, nx)]
@@ -557,6 +557,17 @@
     def spread(self, z):
         super().spread(z)
         self.push(self.rows(self.me.dp, z, 1), 12 + z, self.me.corner)
+
+    def start(self):
+        me = self.me
+        for d in (1, 2, 3):
+            self.push(self.rows(me.dp, me.z, 1), me.z, me.seq(me.far(d)), self.zsem)
+        self.spread(me.z)
+
+    def step(self, d):
+        z = self.me.far(NS - d)
+        self.came(z)
+        self.spread(z)
 
     def groups(self):
         me = self.me
@@ -1021,7 +1032,8 @@
         rcopy(own, own, ts.at[d - 1], tr.at[d - 1], me.seq(me.far(d))).start()
     first.start()
     vectors.start()
-    send_windows(me, 0, clips, xw, xs, xr, xl)
+    for p in range(CL):
+        send_windows(me, p, clips, xw, xs, xr, xl)
     for w in later:
         w.start()
     for d in (1, 2, 3):
@@ -1038,43 +1050,35 @@
         rcopy(part, part, bs.at[n], br.at[n], me.core).start()
 
     rows(0)
-    first.step1()
-    first.step2()
+    for d in (1, 3, 2):
+        first.step(d)
     vectors.plane()
     rows(1)
+    rows(2)
     vectors.diagonal()
-    rows(2)
+    rows(3)
     first.groups()
     vectors.last()
-    rows(3)
+    rows(4)
     vectors.finish()
     spread_vectors(sv, vec)
-    rows(4)
     first.finish()
 
     def first_poll(quad):
+        pass
+
+    def second_poll(quad):
         def second():
             for w in later:
                 w.step2()
 
-        pl.when(quad == 2)(second)
-
-    def second_poll(quad):
-        def last():
-            for w in later:
-                w.last()
-
-        pl.when(quad == 1)(last)
+        pl.when(quad == 1)(second)
 
     for p, poll in enumerate((first_poll, second_poll)):
+        take_windows(me, p, xw, xs, xr, xl)
         if p == 1:
             for w in later:
-                w.corner()
-        take_windows(me, p, xw, xs, xr, xl)
-        if p == 0:
-            for w in later:
                 w.step1()
-            send_windows(me, 1, clips, xw, xs, xr, xl)
             for c in range(CL):
                 send_windows(me, c, cot, dyw, ds_, dr, dl)
         load_tokens(xw, p, x, p)
@@ -1084,13 +1088,17 @@
                 take(bias_rows(n, me.cn), br.at[n])
                 take(bias_rows(n, me.c), bs.at[n])
         attention_forward(p, q, k, v, bg, e, att, inv, poll)
+    for w in later:
+        w.corner()
+    for w in later:
+        w.last()
     gvec[...] = jnp.zeros_like(gvec)
     for w in later:
         w.finish()
     feed_forward(x, att, vec, wp, w1, w2, nm, mid, out, bg)
     for p in range(CL):
         store_tokens(out, order[0, p], xw, p)
-    send_home(me, xw, out_t, os_, or_, ol)
+    send_home(me, range(CL), xw, out_t, os_, or_, ol)
     reds = [
         Reduce(me, n, grad, total_out, rs, rr, *parts[n])
         for n, (grad, total_out) in enumerate(((wq, oq), (wp, op), (w1, o1), (w2, o2)))
@@ -1109,7 +1117,6 @@
     reds[3].plane_part(3)
     middle_backward(dy, att, vec, wp, mid, out, inv, gvec, do)
     reds[1].cores()
-    reds[3].corner()
     reds[2].plane()
 
     def backward_poll(quad, half):
@@ -1117,8 +1124,11 @@
             for n in (2, 1):
                 getattr(reds[n], name)()
 
-        steps = ((0, reds[1].plane), (2, reds[3].line), (4, reds[3].across))
-        steps += ((5, lambda: both("corner")), (7, lambda: both("line")))
+        def start():
+            reds[3].corner()
+            reds[1].plane()
+
+        steps = ((0, start), (5, reds[3].line), (6, lambda: both("corner")), (7, reds[3].across))
         for n, step in steps:
             if half == n % 2:
                 pl.when(quad == n // 2)(step)
@@ -1130,10 +1140,10 @@
     for d in (1, 2, 3):
         rcopy(gvec, vz.at[d - 1], zs.at[d - 1], zr.at[d - 1], me.seq(me.far(d))).start()
     for n in (2, 1):
-        reds[n].across()
+        reds[n].line()
     for p in range(CL):
         store_tokens(out, p, dyw, p)
-    send_home(me, dyw, dx_t, hs, hr, hl)
+    send_home(me, (0,), dyw, dx_t, hs, hr, hl)
     halves = ((0, SEG * 8), (1, SEG * 8))
     for n in range(SEGS):
 
@@ -1163,14 +1173,17 @@
         for m in range(2):
             scatter_rows(first + m * SEG // 2, SEG // 2, bg, e.at[0, 2 * n + m], hi, lo, total)
 
+    reds[0].plane()
     scatter(0)
-    reds[0].plane()
+    for n in (2, 1):
+        reds[n].across()
     scatter(1)
+    reds[0].corner()
     scatter(2)
-    reds[0].corner()
+    reds[0].line()
     scatter(3)
-    reds[0].line()
     scatter(4)
+    reds[0].across()
     sums = total[...].T
     for a in range(TA):
         for s in range(NS):
@@ -1178,7 +1191,7 @@
     tblb[...] = tbl[...].astype(bf)
     for d in (1, 2, 3):
         rcopy(tblb.at[me.far(d)], tz.at[d - 1], zs.at[2 + d], zr.at[2 + d], me.seq(me.far(d))).start()
-    reds[0].across()
+    send_home(me, (1,), dyw, dx_t, hs, hr, hl)
     table = tbl[pl.ds(me.z, 1)].reshape(4, TA * TB)
     vecs = gvec[...]
     for d in (1, 2, 3):

time: 151 us -> 147 us (0.974)
  Pallas kernels: 149 us -> 146 us
    pallas_call x1, Pallas kernels: 147 us -> 143 us  [windowed(): pl.pallas_call(block_kernel, out_shape=outs, in_specs=[spec(pltpu.SMEM)]...]
where the time goes in v2:
time: 147 us
  Pallas kernels  146 us (99%)
    pallas_call x1, Pallas kernels, windowed(): pl.pallas_call(block_kernel, out_shape=outs, in_specs=[spec(pltpu.SMEM)]...  143 us

profile of v2, /device:TPU:0, one launch (start us, length us, event | category | flops | bytes accessed | tf_op | source)
XLA Modules:
  0.0 146.6 jit_solution(4449308959558315748)
XLA Ops:
  0.7 142.8 %shard_map.298 = (bf16[2,14,14,2,512]{4,3,2,1,0:T(2,128)(2,1)}, bf16[2,14,14,2,512]{4,3,2,1,0:T(2,128)(2,1)}, f32[16,1536]{1,0:T(8,128)}, f32[16,512]{1,0:T(8,12...) custom-call(s32[1,2]{1,0:T(1,128)} %order.1, ...), custom_call_target="tpu_custom_call" | custom-call | tf_op jit(solution)/shard_map/pallas_call | solution.py:1269
  143.5 2.9 %shard_map.299 = (bf16[2,14,14,2,512]{4,3,2,1,0:T(2,128)(2,1)}, bf16[2,14,14,2,512]{4,3,2,1,0:T(2,128)(2,1)}, f32[16,1536]{1,0:T(8,128)}, f32[16,512]{1,0:T(8,12...) custom-call(bf16[2,14,14,2,512]{4,3,2,1,0:T(2,128)(2,1)} %get-tuple-, ...), custom_call_target="tpu_custom_call" | custom-call | tf_op jit(solution)/shard_map/pallas_call | solution.py:1295
